TPU v7x, 256 devices: a whole 4x4x8 slice. The times are simulated.
256 devices in a mesh: dom: 64 (over x_lo, y, z), grp: 4 (over x_hi, core).
Axes of the slice: x: 4 (x_hi: 2, x_lo: 2; x = x_hi * 2 + x_lo), y: 4, z: 8, core: 2. Of those that a mesh axis runs over, the one named last changes fastest.
Arguments:
- particles: bfloat16 [114688, 4096], P(('dom', 'grp')), may hold values from -40 to 40
- rot_center: int32 [114688], P(('dom', 'grp')), may hold values from 0 to 29
- shifts: int32 [2, 114688], P(None, ('dom', 'grp')), may hold values from -3 to 3
- references: bfloat16 [32, 30, 4096], P('grp'), may hold values from -3 to 3
- class_prior: float32 [32], replicated, may hold values from 0.0001 to 1
- sigma2: float32 [2048], replicated, may hold values from 10 to 40
Outputs:
- class_means: float32 [32, 122880], P('grp', 'dom')
All inputs are finite; a program needn't handle non-finite values.
Results may differ from a plain program's by a relative error of at most 0.0023.
Values may be sent and summed in bfloat16 or wider, within the bound.
No kernel may reach another device: no remote copies, remote signals or barrier semaphores. Data moves between devices by JAX's collectives and lax.ppermute only.
A program may use at most 128 MiB of HBM per device.

v0:
```python
import functools

import jax
import jax.numpy as jnp
from jax import lax
from jax.experimental import pallas as pl
from jax.experimental.pallas import tpu as pltpu
from jax.sharding import Mesh, PartitionSpec as P

HALFWIN = 6
BOX = 128
KXW = 32
KYW = 64
TWO_PI = 6.283185307179586
REG_WEIGHT = 0.05

F = 2048
WIDE = 2 * F
ROTS = 30
ROWS = ROTS * 8
NP = 448
PAD = 512
NP2 = 2 * PAD
LANES = NP2 // 128
DIRECT = 1024
QUART = 512
ZBASE = DIRECT + 4 * QUART
UNITS = 15
PART = 8
PROWS = PART * 8

BF = jnp.bfloat16
F32 = jnp.float32
MB = 1024 * 1024


def turn_cos_sin(turns):
    quarter = jnp.floor(4.0 * turns + 0.5)
    x = TWO_PI * (turns - 0.25 * quarter)
    q = quarter - 4.0 * jnp.floor(0.25 * quarter)
    x2 = x * x
    s = x * (1.0 + x2 * (-1.0 / 6 + x2 * (1.0 / 120 + x2 * (-1.0 / 5040 + x2 * (1.0 / 362880)))))
    c = 1.0 + x2 * (-0.5 + x2 * (1.0 / 24 + x2 * (-1.0 / 720 + x2 * (1.0 / 40320))))
    odd = (q == 1.0) | (q == 3.0)
    cos = jnp.where(odd, s, c)
    sin = jnp.where(odd, c, s)
    cos = jnp.where((q == 1.0) | (q == 2.0), -cos, cos)
    sin = jnp.where(q >= 2.0, -sin, sin)
    return cos, sin


SHIFT_ROWS = 64
SHIFT_STEPS = NP // SHIFT_ROWS


def shift_kernel(meta_ref, p_ref, o_ref, held_ref, turned_ref, sems):
    def copy(step):
        rows = pl.ds(step * SHIFT_ROWS, SHIFT_ROWS)
        return pltpu.make_async_copy(p_ref.at[rows, :], held_ref.at[rows, :], sems.at[step])

    for step in range(SHIFT_STEPS):
        copy(step).start()
    turned_ref[...] = jnp.transpose(meta_ref[...])
    lane = lax.broadcasted_iota(jnp.int32, (SHIFT_ROWS, 128), 1)
    kx = (lane & (KXW - 1)).astype(F32)
    ky = ((lane >> 5) - KYW // 2).astype(F32)
    for step in range(SHIFT_STEPS):
        rows = slice(step * SHIFT_ROWS, (step + 1) * SHIFT_ROWS)
        sx = turned_ref[rows, 0:1]
        sy = turned_ref[rows, 1:2]
        c, s = turn_cos_sin((sx * kx + sy * ky) * (1.0 / BOX))
        dc, ds = turn_cos_sin(jnp.broadcast_to(sy * (128 // KXW), (SHIFT_ROWS, 128)) * (1.0 / BOX))
        copy(step).wait()
        for b in range(F // 128):
            re = held_ref[rows, b * 128 : (b + 1) * 128].astype(F32)
            im = held_ref[rows, F + b * 128 : F + (b + 1) * 128].astype(F32)
            o_ref[rows, b * 128 : (b + 1) * 128] = (re * c + im * s).astype(BF)
            o_ref[rows, F + b * 128 : F + (b + 1) * 128] = (im * c - re * s).astype(BF)
            c, s = c * dc - s * ds, s * dc + c * ds


def shift_particles(particles, meta, megabytes):
    return pl.pallas_call(
        shift_kernel,
        out_shape=jax.ShapeDtypeStruct((NP, WIDE), BF),
        in_specs=[VMEM, pl.BlockSpec(memory_space=pl.ANY)],
        out_specs=VMEM,
        scratch_shapes=[
            pltpu.VMEM((NP, WIDE), BF),
            pltpu.VMEM((PAD, 8), F32),
            pltpu.SemaphoreType.DMA((SHIFT_STEPS,)),
        ],
        cost_estimate=cost(5),
        compiler_params=pltpu.CompilerParams(vmem_limit_bytes=megabytes * MB),
    )(meta, particles)


def weigh(own_ref, oth_ref, inv_ref, w_ref):
    width = 512
    for start in range(0, WIDE, width):
        cols = slice(start, start + width)
        inv = inv_ref[:, cols]
        w_ref[0:NP, cols] = (own_ref[:, cols].astype(F32) * inv).astype(BF)
        w_ref[PAD : PAD + NP, cols] = (oth_ref[:, cols].astype(F32) * inv).astype(BF)
        w_ref[NP:PAD, cols] = jnp.zeros((PAD - NP, width), BF)
        w_ref[PAD + NP :, cols] = jnp.zeros((PAD - NP, width), BF)


def correlate(w_ref, inv_ref, pieces, acc_ref, begun=None):
    energy = jnp.zeros((ROWS, 128), F32)
    for piece, base, width in pieces:
        for start in range(0, piece.shape[1], width):
            cols = pl.ds(base + start, width)
            inv = inv_ref[:, cols]
            part = lax.dot_general(
                piece[:, start : start + width],
                w_ref[:, cols],
                (((1,), (1,)), ((), ())),
                preferred_element_type=F32,
            )
            for j in range(LANES):
                block = part[:, j * 128 : (j + 1) * 128]
                acc_ref[j] = block if begun is None else begun[j] + block
            begun = acc_ref
            for lanes in range(0, width, 128):
                v = piece[:, start + lanes : start + lanes + 128].astype(F32)
                energy = energy + v * v * inv[:, lanes : lanes + 128]
    return energy


def offset(bias_ref, energy):
    return bias_ref[...] - 0.5 * jnp.sum(energy, axis=1, keepdims=True)


def exponentiate(acc_ref, bias, metas, out_ref, j):
    half = LANES // 2
    rot = metas[j // half][2:3, (j % half) * 128 : (j % half + 1) * 128]
    low = jnp.full((8, 128), -jnp.inf, F32)
    top = low
    for r in range(ROTS):
        rows = slice(r * 8, r * 8 + 8)
        score = jnp.where(inside_window(r, rot), acc_ref[j, rows, :] + bias[rows, :], low)
        out_ref[j, rows, :] = score
        top = jnp.maximum(top, score)
    top = jnp.max(top, axis=0, keepdims=True)
    mass = jnp.zeros((8, 128), F32)
    for r in range(ROTS):
        rows = slice(r * 8, r * 8 + 8)
        raised = jnp.exp(out_ref[j, rows, :] - top)
        out_ref[j, rows, :] = raised
        mass = mass + raised
    return top, jnp.sum(mass, axis=0, keepdims=True)


def inside_window(rotation, rot):
    return jnp.abs(jnp.abs(float(rotation) - rot) - ROTS / 2) >= ROTS / 2 - HALFWIN


def own_kernel(
    where_ref, own_ref, oth_ref, inv_ref, bias_ref, refs_ref, meta_a, meta_b, q0, z0,
    w_ref, e_ref, stats_ref, begun_ref, energy_ref, acc_ref,
):
    weigh(own_ref, oth_ref, inv_ref, w_ref)
    bias = offset(bias_ref, correlate(w_ref, inv_ref, [(refs_ref, 0, 512)], acc_ref))
    pieces = [(q, pl.multiple_of(where_ref[s], 128), QUART) for s, q in enumerate((q0, z0))]
    energy_ref[...] = correlate(w_ref, inv_ref, pieces, begun_ref)
    row = lax.broadcasted_iota(jnp.int32, (8, 128), 0)
    for j in range(LANES):
        top, mass = exponentiate(acc_ref, bias, (meta_a, meta_b), e_ref, j)
        stats_ref[:, j * 128 : (j + 1) * 128] = jnp.where(row == 0, top, mass)


def other_kernel(
    where_ref, w_ref, inv_ref, bias_ref, meta_a, meta_b, first_ref, begun_ref, energy_ref, d_ref, q1, q2, q3, z1,
    e_ref, stats_ref, acc_ref,
):
    pieces = [(d_ref, 0, 512)]
    for s, q in enumerate((q1, q2, q3, z1)):
        pieces.append((q, pl.multiple_of(where_ref[s], 128), QUART))
    bias = offset(bias_ref, energy_ref[...] + correlate(w_ref, inv_ref, pieces, acc_ref, begun_ref))
    row = lax.broadcasted_iota(jnp.int32, (8, 128), 0)
    for j in range(LANES):
        lanes = slice(j * 128, (j + 1) * 128)
        top_b, mass_b = exponentiate(acc_ref, bias, (meta_a, meta_b), e_ref, j)
        top_a, mass_a = first_ref[0:1, lanes], first_ref[1:2, lanes]
        top = jnp.maximum(top_a, top_b)
        mass = mass_a * jnp.exp(top_a - top) + mass_b * jnp.exp(top_b - top)
        tops = jnp.where(row == 2, top_a, top_b)
        stats_ref[:, lanes] = jnp.where(row == 0, top, jnp.where(row == 1, mass, tops))


def sums_kernel(where_ref, first_ref, second_ref, mine_ref, theirs_ref, own_ref, oth_ref, *refs):
    parts, (p_ref, acc_ref, mass_ref, extra_ref) = refs[:8], refs[8:]
    x_hi, x_lo, y, z = where_ref[0], where_ref[1], where_ref[2], where_ref[3]
    mass_ref[...] = jnp.zeros_like(mass_ref)
    for j in range(LANES):
        lanes = slice(j * 128, (j + 1) * 128)
        facing = (j + LANES // 2) % LANES
        crossed = slice(facing * 128, (facing + 1) * 128)
        top_a, mass_a = mine_ref[0:1, lanes], mine_ref[1:2, lanes]
        top_b, mass_b = theirs_ref[0:1, crossed], theirs_ref[1:2, crossed]
        top = jnp.maximum(top_a, top_b)
        scale = 1.0 / (mass_a * jnp.exp(top_a - top) + mass_b * jnp.exp(top_b - top))
        scale_a = jnp.exp(mine_ref[2:3, lanes] - top) * scale
        scale_b = jnp.exp(mine_ref[3:4, lanes] - top) * scale
        if j % (LANES // 2) == LANES // 2 - 1:
            used = lax.broadcasted_iota(jnp.int32, (1, 128), 1) < 128 - (PAD - NP)
            scale_a = jnp.where(used, scale_a, 0.0)
            scale_b = jnp.where(used, scale_b, 0.0)
        for r in range(ROTS):
            rows = slice(r * 8, r * 8 + 8)
            p = first_ref[j, rows, :] * scale_a
            q = second_ref[j, rows, :] * scale_b
            low = jnp.where(x_hi == 0, p, q)
            high = jnp.where(x_hi == 0, q, p)
            both = jnp.concatenate([low, high], axis=0)
            p_ref[r * 16 : (r + 1) * 16, lanes] = both.astype(BF)
            mass_ref[r * 16 : (r + 1) * 16, :] += both
    lane = lax.broadcasted_iota(jnp.int32, (16, 128), 1)
    totals = jnp.zeros((16, 128), F32)
    for r in range(ROTS):
        row_sum = jnp.sum(mass_ref[r * 16 : (r + 1) * 16, :], axis=1, keepdims=True)
        totals = jnp.where(lane == r, row_sum, totals)
    coarse = totals.astype(BF).astype(F32)
    extra_ref[...] = jnp.where(lane < 32, coarse, pltpu.roll(totals - coarse, 32, 1))
    width = 512
    for cb in range(WIDE // width):
        cols = slice(cb * width, (cb + 1) * width)
        part = jnp.dot(p_ref[:, 0:NP], own_ref[:, cols], preferred_element_type=F32) + jnp.dot(
            p_ref[:, PAD : PAD + NP], oth_ref[:, cols], preferred_element_type=F32
        )
        for j in range(width // 128):
            fb = cb * (width // 128) + j
            for r in range(ROTS):
                for kx in range(2):
                    row = r * 16 + kx * 8
                    acc_ref[kx, 32 * r + fb] = part[row : row + 8, j * 128 : (j + 1) * 128]

    def place(sz, carry):
        dest_z = (z + sz) & 7
        for sx in range(4):
            kx, dest_x = x_hi ^ (sx >> 1), x_lo ^ (sx & 1)
            for sy in range(4):
                base = ((dest_x * 4 + ((y + sy) & 3)) * 8 + dest_z) * UNITS

                def tile(i):
                    if i == UNITS:
                        return extra_ref[pl.ds(pl.multiple_of(kx * 8, 8), 8), :]
                    return acc_ref[kx, base + i]

                for i in range(0, UNITS + 1, 2):
                    both = jnp.concatenate([tile(i), tile(i + 1)], axis=0)
                    number = i // PART
                    hop, rest = (sx, sy) if number % 2 == 0 else (sy, sx)
                    row = (i % PART) * 8
                    part_ref = parts[number * 4 + hop]
                    part_ref[rest, sz, row : row + 16, :] = both.astype(part_ref.dtype)
        return carry

    lax.fori_loop(0, 8, place, 0)


def first_sum_kernel(*refs):
    for half in range(2):
        arrived = refs[half:8:2]
        for rest in range(4):
            for z in range(8):
                total = arrived[0][rest, z].astype(F32)
                for ref in arrived[1:]:
                    total = total + ref[rest, z].astype(F32)
                out_ref = refs[8 + 4 * half + rest]
                out_ref[z] = total.astype(out_ref.dtype)


def second_sum_kernel(*refs):
    for half in range(2):
        arrived = refs[half:8:2]
        for z in range(8):
            total = arrived[0][z]
            for ref in arrived[1:]:
                total = total + ref[z].astype(F32)
            refs[8 + z][half * PROWS : (half + 1) * PROWS, :] = total


def final_kernel(where_ref, sigma_ref, *refs):
    d = where_ref[0]
    out_ref = refs[8]

    def rows_of(i):
        rows = slice(i * 8, i * 8 + 8)
        total = refs[0][rows, :]
        for ref in refs[1:8]:
            total = total + ref[rows, :]
        return total

    mass = rows_of(UNITS)
    mass = mass + pltpu.roll(mass, 128 - 32, 1)
    lane = lax.broadcasted_iota(jnp.int32, (8, 128), 1)
    for i in range(UNITS):
        unit = d * UNITS + i
        rotation = unit >> 5
        here = jnp.sum(jnp.where(lane == rotation, mass, 0.0), axis=1, keepdims=True)
        noise = sigma_ref[pl.ds(unit & 15, 1), :]
        out_ref[:, i * 128 : (i + 1) * 128] = rows_of(i) / (here + REG_WEIGHT * noise)


def cost(micros):
    return pl.CostEstimate(flops=int(micros * 1e9), bytes_accessed=0, transcendentals=0)


SMEM = pl.BlockSpec(memory_space=pltpu.SMEM)
VMEM = pl.BlockSpec(memory_space=pltpu.VMEM)


def ring(size, step):
    return [((i + step) % size, i) for i in range(size)]


X = ("x_lo", "x_hi")
X_SWAP = [(0, 3), (1, 2), (2, 1), (3, 0)]
CORE_SWAP = [(0, 1), (1, 0)]


def from_y(value, step):
    return lax.ppermute(value, "y", ring(4, step))


def to_x(value, flips):
    return lax.ppermute(value, X, [(i, i ^ (flips >> 1) ^ ((flips & 1) << 1)) for i in range(4)])


def to_y(value, step):
    return lax.ppermute(value, "y", ring(4, -step))


def to_z(value, step):
    return lax.ppermute(value, "z", ring(8, -step))


def local(particles, rot_center, shifts, references, class_prior, sigma2):
    x_lo, y, z = lax.axis_index("x_lo"), lax.axis_index("y"), lax.axis_index("z")
    x_hi, core = lax.axis_index("x_hi"), lax.axis_index("core")
    refs = jnp.transpose(references, (1, 0, 2)).reshape(ROWS, WIDE)

    zp = z & 1
    with jax.named_scope("swap"):
        raw = lax.ppermute(particles, "core", CORE_SWAP)
    with jax.named_scope("references"):
        quarter = lax.dynamic_slice_in_dim(refs, DIRECT + y * QUART, QUART, 1)
        half = lax.dynamic_slice_in_dim(refs, ZBASE + zp * QUART, QUART, 1)
        quarter, half, shifts, rot_center = lax.optimization_barrier((quarter, half, shifts, rot_center))
        crossed = lax.ppermute(quarter, X, X_SWAP)
    with jax.named_scope("swap"):
        meta = jnp.concatenate([shifts, rot_center[None]]).astype(F32)
        meta = jnp.pad(meta, ((0, 5), (0, PAD - NP)))
        meta_oth = lax.ppermute(meta, "core", CORE_SWAP)
    with jax.named_scope("references"):
        half, meta_oth = lax.optimization_barrier((half, meta_oth))
        z_crossed = lax.ppermute(half, X, X_SWAP)
        later_refs, meta = lax.optimization_barrier((refs, meta))
        direct, meta_oth = lax.optimization_barrier((later_refs[:, :DIRECT], meta_oth))
        direct = lax.ppermute(direct, X, X_SWAP)
    with jax.named_scope("shift"):
        own = shift_particles(particles, meta, 48)
        raw, crossed = lax.optimization_barrier((raw, crossed))
        oth = shift_particles(raw, meta_oth, 12)
    with jax.named_scope("references"):
        quarters = [from_y(crossed, s) for s in (1, 2, 3)]
        z_crossed, oth = lax.optimization_barrier((z_crossed, oth))
        z_other = lax.ppermute(z_crossed, "z", [(i, i ^ 1) for i in range(8)])
    inv = (1.0 / jnp.concatenate([sigma2, sigma2])).reshape(1, WIDE)
    log_prior = jnp.log(class_prior).reshape(2, 2, 8)
    own_bias = jnp.tile(log_prior[x_hi, core], ROTS).reshape(ROWS, 1)
    oth_bias = jnp.tile(log_prior[1 - x_hi, core], ROTS).reshape(ROWS, 1)

    raised = jax.ShapeDtypeStruct((LANES, ROWS, 128), F32)
    stats = jax.ShapeDtypeStruct((8, NP2), F32)
    with jax.named_scope("scores"):
        offsets = [DIRECT + ((y + s) & 3) * QUART for s in range(4)]
        z_offsets = [ZBASE + zp * QUART, ZBASE + (1 - zp) * QUART]
        energies = jax.ShapeDtypeStruct((ROWS, 128), F32)
        weighted, first, first_stats, begun, energy = pl.pallas_call(
            own_kernel,
            out_shape=[jax.ShapeDtypeStruct((NP2, WIDE), BF), raised, stats, raised, energies],
            in_specs=[SMEM] + [VMEM] * 9,
            out_specs=[VMEM] * 5,
            scratch_shapes=[pltpu.VMEM((LANES, ROWS, 128), F32)],
            cost_estimate=cost(7),
            compiler_params=pltpu.CompilerParams(vmem_limit_bytes=6 * MB),
        )(jnp.stack([offsets[0], z_offsets[0]]), own, oth, inv, own_bias, refs, meta, meta_oth, crossed, z_crossed)
        second, mine = pl.pallas_call(
            other_kernel,
            out_shape=[raised, stats],
            in_specs=[SMEM] + [VMEM] * 13,
            out_specs=[VMEM] * 2,
            scratch_shapes=[pltpu.VMEM((LANES, ROWS, 128), F32)],
            cost_estimate=cost(5),
            compiler_params=pltpu.CompilerParams(vmem_limit_bytes=6 * MB),
        )(
            jnp.stack(offsets[1:] + z_offsets[1:]), weighted, inv, oth_bias, meta, meta_oth, first_stats,
            begun, energy, direct, *quarters, z_other,
        )
        theirs = lax.ppermute(mine, "core", CORE_SWAP)

    with jax.named_scope("sums"):
        parts = pl.pallas_call(
            sums_kernel,
            out_shape=([jax.ShapeDtypeStruct((4, 8, PROWS, 128), F32)] + [jax.ShapeDtypeStruct((4, 8, PROWS, 128), BF)] * 3) * 2,
            in_specs=[SMEM] + [VMEM] * 6,
            out_specs=[VMEM] * 8,
            scratch_shapes=[
                pltpu.VMEM((ROTS * 16, NP2), BF),
                pltpu.VMEM((2, ROTS * WIDE // 128, 8, 128), F32),
                pltpu.VMEM((ROTS * 16, 128), F32),
                pltpu.VMEM((16, 128), F32),
            ],
            cost_estimate=cost(6),
            compiler_params=pltpu.CompilerParams(vmem_limit_bytes=14 * MB),
        )(jnp.stack([x_hi, x_lo, y, z]), first, second, mine, theirs, own, oth)

    order = (2, 3, 1)
    sends = (to_x, to_y)
    with jax.named_scope("reduce1"):
        arrived = [[parts[0]], [parts[4]]]
        for s in order:
            for n in range(2):
                arrived[n].append(sends[n](parts[4 * n + s], s))
        firsts = pl.pallas_call(
            first_sum_kernel,
            out_shape=([jax.ShapeDtypeStruct((8, PROWS, 128), F32)] + [jax.ShapeDtypeStruct((8, PROWS, 128), BF)] * 3) * 2,
            in_specs=[VMEM] * 8,
            out_specs=[VMEM] * 8,
            compiler_params=pltpu.CompilerParams(vmem_limit_bytes=4 * MB),
        )(*[piece for pair in zip(*arrived) for piece in pair])
    with jax.named_scope("reduce2"):
        pieces = [[firsts[0]], [firsts[4]]]
        for s in order:
            for n in range(2):
                pieces[n].append(sends[1 - n](firsts[4 * n + s], s))
        slots = pl.pallas_call(
            second_sum_kernel,
            out_shape=[jax.ShapeDtypeStruct((2 * PROWS, 128), F32)] * 8,
            in_specs=[VMEM] * 8,
            out_specs=[VMEM] * 8,
            compiler_params=pltpu.CompilerParams(vmem_limit_bytes=4 * MB),
        )(*[piece for pair in zip(*pieces) for piece in pair])
    with jax.named_scope("reduce3"):
        owned = [slots[0]] + [to_z(slots[s], s) for s in (4, 3, 5, 2, 6, 1, 7)]

    with jax.named_scope("means"):
        d = (x_lo * 4 + y) * 8 + z
        return pl.pallas_call(
            final_kernel,
            out_shape=jax.ShapeDtypeStruct((8, 1920), F32),
            in_specs=[SMEM] + [VMEM] * 9,
            out_specs=VMEM,
            compiler_params=pltpu.CompilerParams(vmem_limit_bytes=4 * MB),
        )(d.reshape(1), sigma2.reshape(16, 128), *owned)


def solution(mesh):
    fine = Mesh(mesh.devices.reshape(2, 4, 8, 2, 2), ("x_lo", "y", "z", "x_hi", "core"))
    dom, grp = ("x_lo", "y", "z"), ("x_hi", "core")
    return jax.shard_map(
        local,
        mesh=fine,
        in_specs=(P(dom + grp, None), P(dom + grp), P(None, dom + grp), P(grp, None, None), P(), P()),
        out_specs=P(grp, dom),
        check_vma=False,
    )
```

profile of v0, /device:TPU:8, one launch (start us, length us, event | category | flops | bytes accessed | tf_op | source)
XLA Modules:
  0.0 106.7 jit_solution(6524057046833305473)
XLA Ops:
  0.0 1.1 %constant_dynamic-slice_fusion.2 = (bf16[240,512]{1,0:T(8,128)(2,1)S(1)}, bf16[240,512]{1,0:T(8,128)(2,1)S(1)}) fusion(bf16[240,4096]{1,0:T(8,128)(2,1)} %bitcast.21, s32[]{:T(128)S(6)} %select_n.17, s32[]{:T(128)S(6)} %select_n.16), kind=kLoop, calls=%fused_computation.4 | loop fusion | bytes 983048 | tf_op jit(solution)/shard_map/references/dynamic_slice | solution.py:350
  1.1 0.7 add_convert_fusion
  1.8 0.6 collective-permute-start
  2.4 2.8 %collective-permute-start.3 = (bf16[240,512]{1,0:T(8,128)(2,1)S(1)}, bf16[240,512]{1,0:T(8,128)(2,1)S(1)}, u32[]{:S(2)}, u32[]{:S(2)}) collective-permute-start(bf16[240,512]{1,0:T(8,128)(2,1)S(1)} %get-tuple-element.58), channel_id=1, source_target_pairs={{0,130},{2,128},{128,2},{130,0},{1,131},{3,129},{129,3},{131,1},{4... | collective-permute-start | bytes 737288 | tf_op jit(solution)/shard_map/references/ppermute | solution.py:352
  5.2 0.8 maximum_divide_fusion.inv_ref
  6.0 4.1 %shift.2.own_ref = bf16[448,4096]{1,0:T(8,128)(2,1)S(1)} custom-call(f32[8,512]{1,0:T(8,128)S(1)} %pad.4.meta_ref.meta_a, bf16[448,4096]{1,0:T(8,128)(2,1)} %p_ref.1), custom_call_target="tpu_custom_call" | custom-call | flops 5000000000 | tf_op jit(solution)/shard_map/shift/pallas_call | solution.py:83
  10.1 1.8 %copy-done.2 = bf16[448,4096]{1,0:T(8,128)(2,1)} copy-done((bf16[448,4096]{1,0:T(8,128)(2,1)}, bf16[448,4096]{1,0:T(8,128)(2,1)S(1)}, u32[]{:S(2)}) %copy-start.2) | copy-done | bytes 3670040
  12.5 0.6 collective-permute-start.1
  13.0 2.8 %collective-permute-start.4 = (bf16[240,1024]{1,0:T(8,128)(2,1)S(1)}, bf16[240,1024]{1,0:T(8,128)(2,1)S(1)}, u32[]{:S(2)}, u32[]{:S(2)}) collective-permute-start(bf16[240,1024]{1,0:T(8,128)(2,1)S(1)} %slice.3), channel_id=1, source_target_pairs={{0,130},{2,128},{128,2},{130,0},{1,131},{3,129},{129,3},{131,1},{4... | collective-permute-start | bytes 1474568 | tf_op jit(solution)/shard_map/references/ppermute | solution.py:362
  15.8 0.5 collective-permute-start.5
  16.2 2.6 %collective-permute-start.6 = (bf16[240,512]{1,0:T(8,128)(2,1)S(1)}, bf16[240,512]{1,0:T(8,128)(2,1)S(1)}, u32[]{:S(2)}, u32[]{:S(2)}) collective-permute-start(bf16[240,512]{1,0:T(8,128)(2,1)S(1)} %collective-permute-done.3.q0), channel_id=1, source_target_pairs={{64,0},{96,32},{0,64},{32,96},{65,1},{97,33},{1,65},{33,97},{66,2}... | collective-permute-start | bytes 737288 | tf_op jit(solution)/shard_map/references/ppermute | solution.py:325
  18.8 1.9 %collective-permute-start.7 = (bf16[240,512]{1,0:T(8,128)(2,1)S(1)}, bf16[240,512]{1,0:T(8,128)(2,1)S(1)}, u32[]{:S(2)}, u32[]{:S(2)}) collective-permute-start(bf16[240,512]{1,0:T(8,128)(2,1)S(1)} %collective-permute-done.3.q0), channel_id=1, source_target_pairs={{96,0},{0,32},{32,64},{64,96},{97,1},{1,33},{33,65},{65,97},{98,2}... | collective-permute-start | bytes 737288 | tf_op jit(solution)/shard_map/references/ppermute | solution.py:325
  20.7 4.0 %shift.3.oth_ref = bf16[448,4096]{1,0:T(8,128)(2,1)S(1)} custom-call(f32[8,512]{1,0:T(8,128)S(1)} %collective-permute-done.meta_ref.meta_b, bf16[448,4096]{1,0:T(8,128)(2,1)} %collective-permute-done.2.p_ref), custom_call_target="tpu_custom_call" | custom-call | flops 5000000000 | tf_op jit(solution)/shard_map/shift/pallas_call | solution.py:83
  24.7 2.2 %collective-permute-start.8 = (bf16[240,512]{1,0:T(8,128)(2,1)S(1)}, bf16[240,512]{1,0:T(8,128)(2,1)S(1)}, u32[]{:S(2)}, u32[]{:S(2)}) collective-permute-start(bf16[240,512]{1,0:T(8,128)(2,1)S(1)} %collective-permute-done.1.z0), channel_id=1, source_target_pairs={{0,4},{4,0},{8,12},{12,8},{16,20},{20,16},{24,28},{28,24},{1,5},{5... | collective-permute-start | bytes 737288 | tf_op jit(solution)/shard_map/references/ppermute | solution.py:370
  26.9 4.7 %scores.2 = (bf16[1024,4096]{1,0:T(8,128)(2,1)S(1)}, f32[8,240,128]{2,1,0:T(8,128)S(1)}, f32[8,1024]{1,0:T(8,128)S(1)}, f32[8,240,128]{2,1,0:T(8,128)S(1)}, f32[240,128]{1,0:T(8,128)S(1)}) custom-call(s32[2]{0:T(128)S(1)} %pad_add_fusion.1.where_ref, bf16[448,4096]{1,0:T(8,128)(2,1)S(1)} %copy-done.3, bf16[448,4096]{1,0:T(8,128)(2,1)S(1)} %shift.3.oth_ref, ...), custom_call_target="tpu_custom_call" | custom-call | flops 7000000000 | tf_op jit(solution)/shard_map/scores/pallas_call | solution.py:382
  31.7 0.3 collective-permute-done.4.d_ref
  32.0 3.0 %scores.3 = (f32[8,240,128]{2,1,0:T(8,128)S(1)}, f32[8,1024]{1,0:T(8,128)S(1)}) custom-call(s32[4]{0:T(128)S(1)} %pad_add_fusion.2.where_ref, bf16[1024,4096]{1,0:T(8,128)(2,1)S(1)} %get-tuple-element.64.w_ref, f32[1,4096]{1,0:T(1,128)S(1)} %maximum_divide_fusion.inv_ref, f32[240,1]{1,0:T(8,128)S(1)} %reshape_tile.9.bias_ref, ...), custom_call_target="tpu_custom_call" | custom-call | flops 5000000000 | tf_op jit(solution)/shard_map/scores/pallas_call | solution.py:391
  35.2 1.1 %collective-permute-done.9.theirs_ref = f32[8,1024]{1,0:T(8,128)S(1)} collective-permute-done((f32[8,1024]{1,0:T(8,128)S(1)}, f32[8,1024]{1,0:T(8,128)S(1)}, u32[]{:S(2)}, u32[]{:S(2)}) %collective-permute-start.9) | collective-permute-done | bytes 32800 | tf_op jit(solution)/shard_map/scores/ppermute | solution.py:403
  36.3 5.4 %sums.1 = (f32[4,8,64,128]{3,2,1,0:T(8,128)S(1)}, bf16[4,8,64,128]{3,2,1,0:T(8,128)(2,1)S(1)}, bf16[4,8,64,128]{3,2,1,0:T(8,128)(2,1)S(1)}, bf16[4,8,64,128]{3,2...) custom-call(s32[4]{0:T(128)S(1)} %pad_add_fusion.where_ref, ...), custom_call_target="tpu_custom_call" | custom-call | flops 6000000000 | tf_op jit(solution)/shard_map/sums/pallas_call | solution.py:406
  41.8 2.4 %collective-permute-start.11 = (bf16[4,8,64,128]{3,2,1,0:T(8,128)(2,1)S(1)}, bf16[4,8,64,128]{3,2,1,0:T(8,128)(2,1)S(1)}, u32[]{:S(2)}, u32[]{:S(2)}) collective-permute-start(bf16[4,8,64,128]{3,2,1,0:T(8,128)(2,1)S(1)} %get-tuple-element.74), channel_id=1, source_target_pairs={{64,0},{96,32},{0,64},{32,96},{65,1},{97,33},{1,65},{33,97},{66,2}... | collective-permute-start | bytes 1572872 | tf_op jit(solution)/shard_map/reduce1/ppermute | solution.py:333
  44.2 1.6 %collective-permute-start.12 = (bf16[4,8,64,128]{3,2,1,0:T(8,128)(2,1)S(1)}, bf16[4,8,64,128]{3,2,1,0:T(8,128)(2,1)S(1)}, u32[]{:S(2)}, u32[]{:S(2)}) collective-permute-start(bf16[4,8,64,128]{3,2,1,0:T(8,128)(2,1)S(1)} %get-tuple-element.75), channel_id=1, source_target_pairs={{0,130},{2,128},{128,2},{130,0},{1,131},{3,129},{129,3},{131,1},{4... | collective-permute-start | bytes 1572872 | tf_op jit(solution)/shard_map/reduce1/ppermute | solution.py:329
  45.7 1.4 %collective-permute-start.13 = (bf16[4,8,64,128]{3,2,1,0:T(8,128)(2,1)S(1)}, bf16[4,8,64,128]{3,2,1,0:T(8,128)(2,1)S(1)}, u32[]{:S(2)}, u32[]{:S(2)}) collective-permute-start(bf16[4,8,64,128]{3,2,1,0:T(8,128)(2,1)S(1)} %get-tuple-element.76), channel_id=1, source_target_pairs={{32,0},{64,32},{96,64},{0,96},{33,1},{65,33},{97,65},{1,97},{34,2}... | collective-permute-start | bytes 1572872 | tf_op jit(solution)/shard_map/reduce1/ppermute | solution.py:333
  47.1 1.8 %collective-permute-start.14 = (bf16[4,8,64,128]{3,2,1,0:T(8,128)(2,1)S(1)}, bf16[4,8,64,128]{3,2,1,0:T(8,128)(2,1)S(1)}, u32[]{:S(2)}, u32[]{:S(2)}) collective-permute-start(bf16[4,8,64,128]{3,2,1,0:T(8,128)(2,1)S(1)} %get-tuple-element.77), channel_id=1, source_target_pairs={{0,128},{2,130},{128,0},{130,2},{1,129},{3,131},{129,1},{131,3},{4... | collective-permute-start | bytes 1572872 | tf_op jit(solution)/shard_map/reduce1/ppermute | solution.py:329
  48.9 9.2 %collective-permute-done.10.refs_2_ = bf16[4,8,64,128]{3,2,1,0:T(8,128)(2,1)S(1)} collective-permute-done((bf16[4,8,64,128]{3,2,1,0:T(8,128)(2,1)S(1)}, bf16[4,8,64,128]{3,2,1,0:T(8,128)(2,1)S(1)}, u32[]{:S(2)}, u32[]{:S(2)}) %collective-permute-start.10) | collective-permute-done | bytes 524320 | tf_op jit(solution)/shard_map/reduce1/ppermute | solution.py:329
  58.1 1.6 %collective-permute-start.15 = (bf16[4,8,64,128]{3,2,1,0:T(8,128)(2,1)S(1)}, bf16[4,8,64,128]{3,2,1,0:T(8,128)(2,1)S(1)}, u32[]{:S(2)}, u32[]{:S(2)}) collective-permute-start(bf16[4,8,64,128]{3,2,1,0:T(8,128)(2,1)S(1)} %get-tuple-element.78), channel_id=1, source_target_pairs={{96,0},{0,32},{32,64},{64,96},{97,1},{1,33},{33,65},{65,97},{98,2}... | collective-permute-start | bytes 1572872 | tf_op jit(solution)/shard_map/reduce1/ppermute | solution.py:333
  59.7 8.8 %collective-permute-done.12.refs_4_ = bf16[4,8,64,128]{3,2,1,0:T(8,128)(2,1)S(1)} collective-permute-done((bf16[4,8,64,128]{3,2,1,0:T(8,128)(2,1)S(1)}, bf16[4,8,64,128]{3,2,1,0:T(8,128)(2,1)S(1)}, u32[]{:S(2)}, u32[]{:S(2)}) %collective-permute-start.12) | collective-permute-done | bytes 524320 | tf_op jit(solution)/shard_map/reduce1/ppermute | solution.py:329
  68.6 1.9 %collective-permute-done.15.refs_7_ = bf16[4,8,64,128]{3,2,1,0:T(8,128)(2,1)S(1)} collective-permute-done((bf16[4,8,64,128]{3,2,1,0:T(8,128)(2,1)S(1)}, bf16[4,8,64,128]{3,2,1,0:T(8,128)(2,1)S(1)}, u32[]{:S(2)}, u32[]{:S(2)}) %collective-permute-start.15) | collective-permute-done | bytes 524320 | tf_op jit(solution)/shard_map/reduce1/ppermute | solution.py:333
  70.5 0.5 reduce1.1
  71.0 2.4 %collective-permute-start.16 = (bf16[8,64,128]{2,1,0:T(8,128)(2,1)S(1)}, bf16[8,64,128]{2,1,0:T(8,128)(2,1)S(1)}, u32[]{:S(2)}, u32[]{:S(2)}) collective-permute-start(bf16[8,64,128]{2,1,0:T(8,128)(2,1)S(1)} %get-tuple-element.81), channel_id=1, source_target_pairs={{64,0},{96,32},{0,64},{32,96},{65,1},{97,33},{1,65},{33,97},{66,2}... | collective-permute-start | bytes 393224 | tf_op jit(solution)/shard_map/reduce2/ppermute | solution.py:333
  73.4 1.3 %collective-permute-start.17 = (bf16[8,64,128]{2,1,0:T(8,128)(2,1)S(1)}, bf16[8,64,128]{2,1,0:T(8,128)(2,1)S(1)}, u32[]{:S(2)}, u32[]{:S(2)}) collective-permute-start(bf16[8,64,128]{2,1,0:T(8,128)(2,1)S(1)} %get-tuple-element.82), channel_id=1, source_target_pairs={{0,2},{2,0},{128,130},{130,128},{1,3},{3,1},{129,131},{131,129},{4... | collective-permute-start | bytes 393224 | tf_op jit(solution)/shard_map/reduce2/ppermute | solution.py:329
  74.6 1.4 %collective-permute-start.18 = (bf16[8,64,128]{2,1,0:T(8,128)(2,1)S(1)}, bf16[8,64,128]{2,1,0:T(8,128)(2,1)S(1)}, u32[]{:S(2)}, u32[]{:S(2)}) collective-permute-start(bf16[8,64,128]{2,1,0:T(8,128)(2,1)S(1)} %get-tuple-element.83), channel_id=1, source_target_pairs={{32,0},{64,32},{96,64},{0,96},{33,1},{65,33},{97,65},{1,97},{34,2}... | collective-permute-start | bytes 393224 | tf_op jit(solution)/shard_map/reduce2/ppermute | solution.py:333
  76.0 0.5 collective-permute-start.19
  76.5 0.7 collective-permute-start.20
  77.1 1.8 %collective-permute-done.16.refs_2_ = bf16[8,64,128]{2,1,0:T(8,128)(2,1)S(1)} collective-permute-done((bf16[8,64,128]{2,1,0:T(8,128)(2,1)S(1)}, bf16[8,64,128]{2,1,0:T(8,128)(2,1)S(1)}, u32[]{:S(2)}, u32[]{:S(2)}) %collective-permute-start.16) | collective-permute-done | bytes 131104 | tf_op jit(solution)/shard_map/reduce2/ppermute | solution.py:333
  78.9 1.0 collective-permute-done.17.refs_3_
  79.9 0.7 collective-permute-done.18.refs_4_
  80.6 1.6 %collective-permute-done.19.refs_5_ = bf16[8,64,128]{2,1,0:T(8,128)(2,1)S(1)} collective-permute-done((bf16[8,64,128]{2,1,0:T(8,128)(2,1)S(1)}, bf16[8,64,128]{2,1,0:T(8,128)(2,1)S(1)}, u32[]{:S(2)}, u32[]{:S(2)}) %collective-permute-start.19) | collective-permute-done | bytes 131104 | tf_op jit(solution)/shard_map/reduce2/ppermute | solution.py:329
  82.2 1.7 %collective-permute-done.21.refs_7_ = bf16[8,64,128]{2,1,0:T(8,128)(2,1)S(1)} collective-permute-done((bf16[8,64,128]{2,1,0:T(8,128)(2,1)S(1)}, bf16[8,64,128]{2,1,0:T(8,128)(2,1)S(1)}, u32[]{:S(2)}, u32[]{:S(2)}) %collective-permute-start.21) | collective-permute-done | bytes 131104 | tf_op jit(solution)/shard_map/reduce2/ppermute | solution.py:329
  83.9 0.1 reduce2.1
  84.0 7.2 %collective-permute-start.22 = (f32[128,128]{1,0:T(8,128)S(1)}, f32[128,128]{1,0:T(8,128)S(1)}, u32[]{:S(2)}, u32[]{:S(2)}) collective-permute-start(f32[128,128]{1,0:T(8,128)S(1)} %get-tuple-element.88), channel_id=1, source_target_pairs={{16,0},{20,4},{24,8},{28,12},{0,16},{4,20},{8,24},{12,28},{17,1},{... | collective-permute-start | bytes 196616 | tf_op jit(solution)/shard_map/reduce3/ppermute | solution.py:337
  91.2 2.0 %collective-permute-start.23 = (f32[128,128]{1,0:T(8,128)S(1)}, f32[128,128]{1,0:T(8,128)S(1)}, u32[]{:S(2)}, u32[]{:S(2)}) collective-permute-start(f32[128,128]{1,0:T(8,128)S(1)} %get-tuple-element.89), channel_id=1, source_target_pairs={{20,0},{24,4},{28,8},{0,12},{4,16},{8,20},{12,24},{16,28},{21,1},{... | collective-permute-start | bytes 196616 | tf_op jit(solution)/shard_map/reduce3/ppermute | solution.py:337
  93.2 3.1 %collective-permute-start.24 = (f32[128,128]{1,0:T(8,128)S(1)}, f32[128,128]{1,0:T(8,128)S(1)}, u32[]{:S(2)}, u32[]{:S(2)}) collective-permute-start(f32[128,128]{1,0:T(8,128)S(1)} %get-tuple-element.90), channel_id=1, source_target_pairs={{12,0},{16,4},{20,8},{24,12},{28,16},{0,20},{4,24},{8,28},{13,1},{... | collective-permute-start | bytes 196616 | tf_op jit(solution)/shard_map/reduce3/ppermute | solution.py:337
  96.2 1.5 %collective-permute-start.25 = (f32[128,128]{1,0:T(8,128)S(1)}, f32[128,128]{1,0:T(8,128)S(1)}, u32[]{:S(2)}, u32[]{:S(2)}) collective-permute-start(f32[128,128]{1,0:T(8,128)S(1)} %get-tuple-element.91), channel_id=1, source_target_pairs={{24,0},{28,4},{0,8},{4,12},{8,16},{12,20},{16,24},{20,28},{25,1},{... | collective-permute-start | bytes 196616 | tf_op jit(solution)/shard_map/reduce3/ppermute | solution.py:337
  97.7 2.7 %collective-permute-start.26 = (f32[128,128]{1,0:T(8,128)S(1)}, f32[128,128]{1,0:T(8,128)S(1)}, u32[]{:S(2)}, u32[]{:S(2)}) collective-permute-start(f32[128,128]{1,0:T(8,128)S(1)} %get-tuple-element.92), channel_id=1, source_target_pairs={{8,0},{12,4},{16,8},{20,12},{24,16},{28,20},{0,24},{4,28},{9,1},{1... | collective-permute-start | bytes 196616 | tf_op jit(solution)/shard_map/reduce3/ppermute | solution.py:337
  100.4 1.0 collective-permute-start.27
  101.4 2.2 %collective-permute-start.28 = (f32[128,128]{1,0:T(8,128)S(1)}, f32[128,128]{1,0:T(8,128)S(1)}, u32[]{:S(2)}, u32[]{:S(2)}) collective-permute-start(f32[128,128]{1,0:T(8,128)S(1)} %get-tuple-element.94), channel_id=1, source_target_pairs={{4,0},{8,4},{12,8},{16,12},{20,16},{24,20},{28,24},{0,28},{5,1},{9... | collective-permute-start | bytes 196616 | tf_op jit(solution)/shard_map/reduce3/ppermute | solution.py:337
  103.6 2.2 %collective-permute-done.27.refs_6_ = f32[128,128]{1,0:T(8,128)S(1)} collective-permute-done((f32[128,128]{1,0:T(8,128)S(1)}, f32[128,128]{1,0:T(8,128)S(1)}, u32[]{:S(2)}, u32[]{:S(2)}) %collective-permute-start.27) | collective-permute-done | bytes 65568 | tf_op jit(solution)/shard_map/reduce3/ppermute | solution.py:337
  105.9 0.8 means.1
  (43 shorter events, 0.9 us)
Async XLA Ops:
  0.0 15.8 %collective-permute-start.2 = (bf16[448,4096]{1,0:T(8,128)(2,1)}, bf16[448,4096]{1,0:T(8,128)(2,1)}, u32[]{:S(2)}, u32[]{:S(2)}) collective-permute-start(bf16[448,4096]{1,0:T(8,128)(2,1)} %p_ref.1), channel_id=1, source_target_pairs={{0,1},{1,0},{2,3},{3,2},{4,5},{5,4},{6,7},{7,6},{8,9},{9,8},{10,11... | collective-permute-start | bytes 11010056 | tf_op jit(solution)/shard_map/swap/ppermute | solution.py:347
  1.8 10.6 %collective-permute-start = (f32[8,512]{1,0:T(8,128)S(1)}, f32[8,512]{1,0:T(8,128)S(1)}, u32[]{:S(2)}, u32[]{:S(2)}) collective-permute-start(f32[8,512]{1,0:T(8,128)S(1)} %pad.4.meta_ref.meta_a), channel_id=1, source_target_pairs={{0,1},{1,0},{2,3},{3,2},{4,5},{5,4},{6,7},{7,6},{8,9},{9,8},{10,11... | collective-permute-start | bytes 49160 | tf_op jit(solution)/shard_map/swap/ppermute | solution.py:356
  2.4 13.4 %collective-permute-start.3 = (bf16[240,512]{1,0:T(8,128)(2,1)S(1)}, bf16[240,512]{1,0:T(8,128)(2,1)S(1)}, u32[]{:S(2)}, u32[]{:S(2)}) collective-permute-start(bf16[240,512]{1,0:T(8,128)(2,1)S(1)} %get-tuple-element.58), channel_id=1, source_target_pairs={{0,130},{2,128},{128,2},{130,0},{1,131},{3,129},{129,3},{131,1},{4... | collective-permute-start | bytes 737288 | tf_op jit(solution)/shard_map/references/ppermute | solution.py:352
  6.0 6.0 %copy-start.4 = (f32[32]{0:T(128)S(1)}, f32[32]{0:T(128)}, u32[]{:S(2)}) copy-start(f32[32]{0:T(128)} %param.10) | copy-start | bytes 388
  6.0 6.2 %copy-start = (bf16[8,30,4096]{2,0,1:T(8,128)(2,1)S(1)}, bf16[8,30,4096]{2,0,1:T(8,128)(2,1)}, u32[]{:S(2)}) copy-start(bf16[8,30,4096]{2,0,1:T(8,128)(2,1)} %param.9) | copy-start | bytes 5898244
  10.1 1.8 %copy-start.2 = (bf16[448,4096]{1,0:T(8,128)(2,1)}, bf16[448,4096]{1,0:T(8,128)(2,1)S(1)}, u32[]{:S(2)}) copy-start(bf16[448,4096]{1,0:T(8,128)(2,1)S(1)} %shift.2.own_ref) | copy-start | bytes 11010052
  12.4 14.5 %copy-start.3 = (bf16[448,4096]{1,0:T(8,128)(2,1)S(1)}, bf16[448,4096]{1,0:T(8,128)(2,1)}, u32[]{:S(2)}) copy-start(bf16[448,4096]{1,0:T(8,128)(2,1)} %copy-done.2) | copy-start | bytes 11010052
  12.5 12.3 %collective-permute-start.1 = (bf16[240,512]{1,0:T(8,128)(2,1)S(1)}, bf16[240,512]{1,0:T(8,128)(2,1)S(1)}, u32[]{:S(2)}, u32[]{:S(2)}) collective-permute-start(bf16[240,512]{1,0:T(8,128)(2,1)S(1)} %get-tuple-element.54), channel_id=1, source_target_pairs={{0,130},{2,128},{128,2},{130,0},{1,131},{3,129},{129,3},{131,1},{4... | collective-permute-start | bytes 737288 | tf_op jit(solution)/shard_map/references/ppermute | solution.py:359
  13.0 18.9 %collective-permute-start.4 = (bf16[240,1024]{1,0:T(8,128)(2,1)S(1)}, bf16[240,1024]{1,0:T(8,128)(2,1)S(1)}, u32[]{:S(2)}, u32[]{:S(2)}) collective-permute-start(bf16[240,1024]{1,0:T(8,128)(2,1)S(1)} %slice.3), channel_id=1, source_target_pairs={{0,130},{2,128},{128,2},{130,0},{1,131},{3,129},{129,3},{131,1},{4... | collective-permute-start | bytes 1474568 | tf_op jit(solution)/shard_map/references/ppermute | solution.py:362
  15.8 16.2 %collective-permute-start.5 = (bf16[240,512]{1,0:T(8,128)(2,1)S(1)}, bf16[240,512]{1,0:T(8,128)(2,1)S(1)}, u32[]{:S(2)}, u32[]{:S(2)}) collective-permute-start(bf16[240,512]{1,0:T(8,128)(2,1)S(1)} %collective-permute-done.3.q0), channel_id=1, source_target_pairs={{32,0},{64,32},{96,64},{0,96},{33,1},{65,33},{97,65},{1,97},{34,2}... | collective-permute-start | bytes 737288 | tf_op jit(solution)/shard_map/references/ppermute | solution.py:325
  16.2 15.7 %collective-permute-start.6 = (bf16[240,512]{1,0:T(8,128)(2,1)S(1)}, bf16[240,512]{1,0:T(8,128)(2,1)S(1)}, u32[]{:S(2)}, u32[]{:S(2)}) collective-permute-start(bf16[240,512]{1,0:T(8,128)(2,1)S(1)} %collective-permute-done.3.q0), channel_id=1, source_target_pairs={{64,0},{96,32},{0,64},{32,96},{65,1},{97,33},{1,65},{33,97},{66,2}... | collective-permute-start | bytes 737288 | tf_op jit(solution)/shard_map/references/ppermute | solution.py:325
  18.8 13.1 %collective-permute-start.7 = (bf16[240,512]{1,0:T(8,128)(2,1)S(1)}, bf16[240,512]{1,0:T(8,128)(2,1)S(1)}, u32[]{:S(2)}, u32[]{:S(2)}) collective-permute-start(bf16[240,512]{1,0:T(8,128)(2,1)S(1)} %collective-permute-done.3.q0), channel_id=1, source_target_pairs={{96,0},{0,32},{32,64},{64,96},{97,1},{1,33},{33,65},{65,97},{98,2}... | collective-permute-start | bytes 737288 | tf_op jit(solution)/shard_map/references/ppermute | solution.py:325
  24.7 7.3 %collective-permute-start.8 = (bf16[240,512]{1,0:T(8,128)(2,1)S(1)}, bf16[240,512]{1,0:T(8,128)(2,1)S(1)}, u32[]{:S(2)}, u32[]{:S(2)}) collective-permute-start(bf16[240,512]{1,0:T(8,128)(2,1)S(1)} %collective-permute-done.1.z0), channel_id=1, source_target_pairs={{0,4},{4,0},{8,12},{12,8},{16,20},{20,16},{24,28},{28,24},{1,5},{5... | collective-permute-start | bytes 737288 | tf_op jit(solution)/shard_map/references/ppermute | solution.py:370
  35.0 1.3 %collective-permute-start.9 = (f32[8,1024]{1,0:T(8,128)S(1)}, f32[8,1024]{1,0:T(8,128)S(1)}, u32[]{:S(2)}, u32[]{:S(2)}) collective-permute-start(f32[8,1024]{1,0:T(8,128)S(1)} %get-tuple-element.70.mine_ref), channel_id=1, source_target_pairs={{0,1},{1,0},{2,3},{3,2},{4,5},{5,4},{6,7},{7,6},{8,9},{9,8},{10,11... | collective-permute-start | bytes 98312 | tf_op jit(solution)/shard_map/scores/ppermute | solution.py:403
  41.7 64.2 %copy-start.1 = (f32[2048]{0:T(1024)S(1)}, f32[2048]{0:T(1024)}, u32[]{:S(2)}) copy-start(f32[2048]{0:T(1024)} %param.11) | copy-start | bytes 24580
  41.7 16.4 %collective-permute-start.10 = (bf16[4,8,64,128]{3,2,1,0:T(8,128)(2,1)S(1)}, bf16[4,8,64,128]{3,2,1,0:T(8,128)(2,1)S(1)}, u32[]{:S(2)}, u32[]{:S(2)}) collective-permute-start(bf16[4,8,64,128]{3,2,1,0:T(8,128)(2,1)S(1)} %get-tuple-element.73), channel_id=1, source_target_pairs={{0,2},{2,0},{128,130},{130,128},{1,3},{3,1},{129,131},{131,129},{4... | collective-permute-start | bytes 1572872 | tf_op jit(solution)/shard_map/reduce1/ppermute | solution.py:329
  41.8 17.9 %collective-permute-start.11 = (bf16[4,8,64,128]{3,2,1,0:T(8,128)(2,1)S(1)}, bf16[4,8,64,128]{3,2,1,0:T(8,128)(2,1)S(1)}, u32[]{:S(2)}, u32[]{:S(2)}) collective-permute-start(bf16[4,8,64,128]{3,2,1,0:T(8,128)(2,1)S(1)} %get-tuple-element.74), channel_id=1, source_target_pairs={{64,0},{96,32},{0,64},{32,96},{65,1},{97,33},{1,65},{33,97},{66,2}... | collective-permute-start | bytes 1572872 | tf_op jit(solution)/shard_map/reduce1/ppermute | solution.py:333
  44.2 24.3 %collective-permute-start.12 = (bf16[4,8,64,128]{3,2,1,0:T(8,128)(2,1)S(1)}, bf16[4,8,64,128]{3,2,1,0:T(8,128)(2,1)S(1)}, u32[]{:S(2)}, u32[]{:S(2)}) collective-permute-start(bf16[4,8,64,128]{3,2,1,0:T(8,128)(2,1)S(1)} %get-tuple-element.75), channel_id=1, source_target_pairs={{0,130},{2,128},{128,2},{130,0},{1,131},{3,129},{129,3},{131,1},{4... | collective-permute-start | bytes 1572872 | tf_op jit(solution)/shard_map/reduce1/ppermute | solution.py:329
  45.7 22.9 %collective-permute-start.13 = (bf16[4,8,64,128]{3,2,1,0:T(8,128)(2,1)S(1)}, bf16[4,8,64,128]{3,2,1,0:T(8,128)(2,1)S(1)}, u32[]{:S(2)}, u32[]{:S(2)}) collective-permute-start(bf16[4,8,64,128]{3,2,1,0:T(8,128)(2,1)S(1)} %get-tuple-element.76), channel_id=1, source_target_pairs={{32,0},{64,32},{96,64},{0,96},{33,1},{65,33},{97,65},{1,97},{34,2}... | collective-permute-start | bytes 1572872 | tf_op jit(solution)/shard_map/reduce1/ppermute | solution.py:333
  47.1 21.5 %collective-permute-start.14 = (bf16[4,8,64,128]{3,2,1,0:T(8,128)(2,1)S(1)}, bf16[4,8,64,128]{3,2,1,0:T(8,128)(2,1)S(1)}, u32[]{:S(2)}, u32[]{:S(2)}) collective-permute-start(bf16[4,8,64,128]{3,2,1,0:T(8,128)(2,1)S(1)} %get-tuple-element.77), channel_id=1, source_target_pairs={{0,128},{2,130},{128,0},{130,2},{1,129},{3,131},{129,1},{131,3},{4... | collective-permute-start | bytes 1572872 | tf_op jit(solution)/shard_map/reduce1/ppermute | solution.py:329
  58.1 12.4 %collective-permute-start.15 = (bf16[4,8,64,128]{3,2,1,0:T(8,128)(2,1)S(1)}, bf16[4,8,64,128]{3,2,1,0:T(8,128)(2,1)S(1)}, u32[]{:S(2)}, u32[]{:S(2)}) collective-permute-start(bf16[4,8,64,128]{3,2,1,0:T(8,128)(2,1)S(1)} %get-tuple-element.78), channel_id=1, source_target_pairs={{96,0},{0,32},{32,64},{64,96},{97,1},{1,33},{33,65},{65,97},{98,2}... | collective-permute-start | bytes 1572872 | tf_op jit(solution)/shard_map/reduce1/ppermute | solution.py:333
  71.0 7.9 %collective-permute-start.16 = (bf16[8,64,128]{2,1,0:T(8,128)(2,1)S(1)}, bf16[8,64,128]{2,1,0:T(8,128)(2,1)S(1)}, u32[]{:S(2)}, u32[]{:S(2)}) collective-permute-start(bf16[8,64,128]{2,1,0:T(8,128)(2,1)S(1)} %get-tuple-element.81), channel_id=1, source_target_pairs={{64,0},{96,32},{0,64},{32,96},{65,1},{97,33},{1,65},{33,97},{66,2}... | collective-permute-start | bytes 393224 | tf_op jit(solution)/shard_map/reduce2/ppermute | solution.py:333
  73.4 6.6 %collective-permute-start.17 = (bf16[8,64,128]{2,1,0:T(8,128)(2,1)S(1)}, bf16[8,64,128]{2,1,0:T(8,128)(2,1)S(1)}, u32[]{:S(2)}, u32[]{:S(2)}) collective-permute-start(bf16[8,64,128]{2,1,0:T(8,128)(2,1)S(1)} %get-tuple-element.82), channel_id=1, source_target_pairs={{0,2},{2,0},{128,130},{130,128},{1,3},{3,1},{129,131},{131,129},{4... | collective-permute-start | bytes 393224 | tf_op jit(solution)/shard_map/reduce2/ppermute | solution.py:329
  74.6 6.0 %collective-permute-start.18 = (bf16[8,64,128]{2,1,0:T(8,128)(2,1)S(1)}, bf16[8,64,128]{2,1,0:T(8,128)(2,1)S(1)}, u32[]{:S(2)}, u32[]{:S(2)}) collective-permute-start(bf16[8,64,128]{2,1,0:T(8,128)(2,1)S(1)} %get-tuple-element.83), channel_id=1, source_target_pairs={{32,0},{64,32},{96,64},{0,96},{33,1},{65,33},{97,65},{1,97},{34,2}... | collective-permute-start | bytes 393224 | tf_op jit(solution)/shard_map/reduce2/ppermute | solution.py:333
  76.0 6.2 %collective-permute-start.19 = (bf16[8,64,128]{2,1,0:T(8,128)(2,1)S(1)}, bf16[8,64,128]{2,1,0:T(8,128)(2,1)S(1)}, u32[]{:S(2)}, u32[]{:S(2)}) collective-permute-start(bf16[8,64,128]{2,1,0:T(8,128)(2,1)S(1)} %get-tuple-element.84), channel_id=1, source_target_pairs={{0,130},{2,128},{128,2},{130,0},{1,131},{3,129},{129,3},{131,1},{4... | collective-permute-start | bytes 393224 | tf_op jit(solution)/shard_map/reduce2/ppermute | solution.py:329
  76.5 5.7 %collective-permute-start.20 = (bf16[8,64,128]{2,1,0:T(8,128)(2,1)S(1)}, bf16[8,64,128]{2,1,0:T(8,128)(2,1)S(1)}, u32[]{:S(2)}, u32[]{:S(2)}) collective-permute-start(bf16[8,64,128]{2,1,0:T(8,128)(2,1)S(1)} %get-tuple-element.85), channel_id=1, source_target_pairs={{96,0},{0,32},{32,64},{64,96},{97,1},{1,33},{33,65},{65,97},{98,2}... | collective-permute-start | bytes 393224 | tf_op jit(solution)/shard_map/reduce2/ppermute | solution.py:333
  78.9 5.0 %collective-permute-start.21 = (bf16[8,64,128]{2,1,0:T(8,128)(2,1)S(1)}, bf16[8,64,128]{2,1,0:T(8,128)(2,1)S(1)}, u32[]{:S(2)}, u32[]{:S(2)}) collective-permute-start(bf16[8,64,128]{2,1,0:T(8,128)(2,1)S(1)} %get-tuple-element.86), channel_id=1, source_target_pairs={{0,128},{2,130},{128,0},{130,2},{1,129},{3,131},{129,1},{131,3},{4... | collective-permute-start | bytes 393224 | tf_op jit(solution)/shard_map/reduce2/ppermute | solution.py:329
  84.0 16.4 %collective-permute-start.22 = (f32[128,128]{1,0:T(8,128)S(1)}, f32[128,128]{1,0:T(8,128)S(1)}, u32[]{:S(2)}, u32[]{:S(2)}) collective-permute-start(f32[128,128]{1,0:T(8,128)S(1)} %get-tuple-element.88), channel_id=1, source_target_pairs={{16,0},{20,4},{24,8},{28,12},{0,16},{4,20},{8,24},{12,28},{17,1},{... | collective-permute-start | bytes 196616 | tf_op jit(solution)/shard_map/reduce3/ppermute | solution.py:337
  91.2 10.2 %collective-permute-start.23 = (f32[128,128]{1,0:T(8,128)S(1)}, f32[128,128]{1,0:T(8,128)S(1)}, u32[]{:S(2)}, u32[]{:S(2)}) collective-permute-start(f32[128,128]{1,0:T(8,128)S(1)} %get-tuple-element.89), channel_id=1, source_target_pairs={{20,0},{24,4},{28,8},{0,12},{4,16},{8,20},{12,24},{16,28},{21,1},{... | collective-permute-start | bytes 196616 | tf_op jit(solution)/shard_map/reduce3/ppermute | solution.py:337
  93.2 10.5 %collective-permute-start.24 = (f32[128,128]{1,0:T(8,128)S(1)}, f32[128,128]{1,0:T(8,128)S(1)}, u32[]{:S(2)}, u32[]{:S(2)}) collective-permute-start(f32[128,128]{1,0:T(8,128)S(1)} %get-tuple-element.90), channel_id=1, source_target_pairs={{12,0},{16,4},{20,8},{24,12},{28,16},{0,20},{4,24},{8,28},{13,1},{... | collective-permute-start | bytes 196616 | tf_op jit(solution)/shard_map/reduce3/ppermute | solution.py:337
  96.2 7.4 %collective-permute-start.25 = (f32[128,128]{1,0:T(8,128)S(1)}, f32[128,128]{1,0:T(8,128)S(1)}, u32[]{:S(2)}, u32[]{:S(2)}) collective-permute-start(f32[128,128]{1,0:T(8,128)S(1)} %get-tuple-element.91), channel_id=1, source_target_pairs={{24,0},{28,4},{0,8},{4,12},{8,16},{12,20},{16,24},{20,28},{25,1},{... | collective-permute-start | bytes 196616 | tf_op jit(solution)/shard_map/reduce3/ppermute | solution.py:337
  97.7 5.9 %collective-permute-start.26 = (f32[128,128]{1,0:T(8,128)S(1)}, f32[128,128]{1,0:T(8,128)S(1)}, u32[]{:S(2)}, u32[]{:S(2)}) collective-permute-start(f32[128,128]{1,0:T(8,128)S(1)} %get-tuple-element.92), channel_id=1, source_target_pairs={{8,0},{12,4},{16,8},{20,12},{24,16},{28,20},{0,24},{4,28},{9,1},{1... | collective-permute-start | bytes 196616 | tf_op jit(solution)/shard_map/reduce3/ppermute | solution.py:337
  100.4 5.5 %collective-permute-start.27 = (f32[128,128]{1,0:T(8,128)S(1)}, f32[128,128]{1,0:T(8,128)S(1)}, u32[]{:S(2)}, u32[]{:S(2)}) collective-permute-start(f32[128,128]{1,0:T(8,128)S(1)} %get-tuple-element.93), channel_id=1, source_target_pairs={{28,0},{0,4},{4,8},{8,12},{12,16},{16,20},{20,24},{24,28},{29,1},{... | collective-permute-start | bytes 196616 | tf_op jit(solution)/shard_map/reduce3/ppermute | solution.py:337
  101.4 4.5 %collective-permute-start.28 = (f32[128,128]{1,0:T(8,128)S(1)}, f32[128,128]{1,0:T(8,128)S(1)}, u32[]{:S(2)}, u32[]{:S(2)}) collective-permute-start(f32[128,128]{1,0:T(8,128)S(1)} %get-tuple-element.94), channel_id=1, source_target_pairs={{4,0},{8,4},{12,8},{16,12},{20,16},{24,20},{28,24},{0,28},{5,1},{9... | collective-permute-start | bytes 196616 | tf_op jit(solution)/shard_map/reduce3/ppermute | solution.py:337
where the time goes:
time: 107 us
  starting transfers between devices  48.5 us (45%)
  waiting for transfers between devices  30.4 us (28%)
  Pallas kernels  22.6 us (21%)
  local copies, waits for them, and re-layouts  3.23 us (3%)
  other arithmetic  1.75 us (2%)
    ppermute x6, waiting for transfers between devices, to_x(): lax.ppermute(value, X, [(i, i ^ flips >> 1 ^ (flips & 1) << 1) for i in r...  22.3 us
    ppermute x7, starting transfers between devices, to_z(): return lax.ppermute(value, 'z', ring(8, -step))  19.6 us
    ppermute x6, starting transfers between devices, to_y(): return lax.ppermute(value, 'y', ring(4, -step))  9.75 us
    pallas_call x2, Pallas kernels, shift_particles(): pl.pallas_call(shift_kernel, out_shape=jax.ShapeDtypeStruct((NP, WIDE), B...  8.1 us
    pallas_call x1, Pallas kernels, local(): pl.pallas_call(sums_kernel, out_shape=([jax.ShapeDtypeStruct((4, 8, PROWS...  5.38 us
    ppermute x6, starting transfers between devices, to_x(): lax.ppermute(value, X, [(i, i ^ flips >> 1 ^ (flips & 1) << 1) for i in r...  5.23 us
    ppermute x3, starting transfers between devices, from_y(): return lax.ppermute(value, 'y', ring(4, step))  4.93 us
    pallas_call x1, Pallas kernels, local(): pl.pallas_call(own_kernel, out_shape=[jax.ShapeDtypeStruct((NP2, WIDE), B...  4.75 us
  transfers between devices with their start and end apart: 29, of which 12 were waited for; matrix products, arithmetic and copies ran while one was open for 3% of the time, Pallas kernels for 12%

commit v1 on v0

--- a/solution.py
+++ b/solution.py
@@ -355,7 +355,7 @@
         meta = jnp.pad(meta, ((0, 5), (0, PAD - NP)))
         meta_oth = lax.ppermute(meta, "core", CORE_SWAP)
     with jax.named_scope("references"):
-        half, meta_oth = lax.optimization_barrier((half, meta_oth))
+        half, meta, meta_oth = lax.optimization_barrier((half, meta, meta_oth))
         z_crossed = lax.ppermute(half, X, X_SWAP)
         later_refs, meta = lax.optimization_barrier((refs, meta))
         direct, meta_oth = lax.optimization_barrier((later_refs[:, :DIRECT], meta_oth))

time: 107 us -> 108 us (level); the launches traced: 107 us -> 106 us
  starting transfers between devices: 48.5 us -> 47.3 us
    ppermute x6, starting transfers between devices: 9.75 us -> 6.41 us  [to_y(): return lax.ppermute(value, 'y', ring(4, -step))]
    ppermute x6, starting transfers between devices: 5.23 us -> 7.39 us  [to_x(): lax.ppermute(value, X, [(i, i ^ flips >> 1 ^ (flips & 1) << 1) for i in r...]
    unnamed x10 -> x4, local copies, waits for them, and re-layouts: 1.81 us -> 0.01 us
    ppermute x1, starting transfers between devices: 0.56 us -> 2.07 us  [local(): z_crossed = lax.ppermute(half, X, X_SWAP)]
    ppermute x1, starting transfers between devices: 2.76 us -> 1.34 us  [local(): direct = lax.ppermute(direct, X, X_SWAP)]
    ppermute x6, waiting for transfers between devices: 4.39 us -> 5.58 us  [to_y(): return lax.ppermute(value, 'y', ring(4, -step))]
  transfers between devices with their start and end apart: 29 -> 29, of which waited for: 12 -> 12; matrix products, arithmetic and copies ran while one was open for 3% -> 5% of each run, Pallas kernels for 12% -> 12%
where the time goes in v1:
time: 108 us; the launch traced here: 106 us
  starting transfers between devices  47.3 us (44%)
  waiting for transfers between devices  31.2 us (29%)
  Pallas kernels  22.2 us (21%)
  local copies, waits for them, and re-layouts  3.12 us (3%)
  other arithmetic  1.75 us (2%)
    ppermute x6, waiting for transfers between devices, to_x(): lax.ppermute(value, X, [(i, i ^ flips >> 1 ^ (flips & 1) << 1) for i in r...  22.3 us
    ppermute x7, starting transfers between devices, to_z(): return lax.ppermute(value, 'z', ring(8, -step))  19.4 us
    pallas_call x2, Pallas kernels, shift_particles(): pl.pallas_call(shift_kernel, out_shape=jax.ShapeDtypeStruct((NP, WIDE), B...  7.94 us
    ppermute x6, starting transfers between devices, to_x(): lax.ppermute(value, X, [(i, i ^ flips >> 1 ^ (flips & 1) << 1) for i in r...  7.39 us
    ppermute x6, starting transfers between devices, to_y(): return lax.ppermute(value, 'y', ring(4, -step))  6.41 us
    ppermute x6, waiting for transfers between devices, to_y(): return lax.ppermute(value, 'y', ring(4, -step))  5.58 us
    pallas_call x1, Pallas kernels, local(): pl.pallas_call(sums_kernel, out_shape=([jax.ShapeDtypeStruct((4, 8, PROWS...  5.32 us
    ppermute x3, starting transfers between devices, from_y(): return lax.ppermute(value, 'y', ring(4, step))  5 us
  transfers between devices with their start and end apart: 29, of which 12 were waited for; matrix products, arithmetic and copies ran while one was open for 5% of the time, Pallas kernels for 12%

profile of v1, /device:TPU:8, one launch (start us, length us, event | category | flops | bytes accessed | tf_op | source)
XLA Modules:
  0.0 105.7 jit_solution(12442957709112730793)
XLA Ops:
  0.0 1.1 %constant_dynamic-slice_fusion.2 = (bf16[240,512]{1,0:T(8,128)(2,1)S(1)}, bf16[240,512]{1,0:T(8,128)(2,1)S(1)}) fusion(bf16[240,4096]{1,0:T(8,128)(2,1)} %bitcast.21, s32[]{:T(128)S(6)} %select_n.17, s32[]{:T(128)S(6)} %select_n.16), kind=kLoop, calls=%fused_computation.4 | loop fusion | bytes 983048 | tf_op jit(solution)/shard_map/references/dynamic_slice | solution.py:350
  1.1 0.7 add_convert_fusion
  1.8 0.6 collective-permute-start
  2.4 2.8 %collective-permute-start.3 = (bf16[240,512]{1,0:T(8,128)(2,1)S(1)}, bf16[240,512]{1,0:T(8,128)(2,1)S(1)}, u32[]{:S(2)}, u32[]{:S(2)}) collective-permute-start(bf16[240,512]{1,0:T(8,128)(2,1)S(1)} %get-tuple-element.60), channel_id=1, source_target_pairs={{0,130},{2,128},{128,2},{130,0},{1,131},{3,129},{129,3},{131,1},{4... | collective-permute-start | bytes 737288 | tf_op jit(solution)/shard_map/references/ppermute | solution.py:352
  5.2 0.7 log.3
  6.0 0.8 maximum_divide_fusion.inv_ref
  7.1 2.1 %collective-permute-start.1 = (bf16[240,512]{1,0:T(8,128)(2,1)S(1)}, bf16[240,512]{1,0:T(8,128)(2,1)S(1)}, u32[]{:S(2)}, u32[]{:S(2)}) collective-permute-start(bf16[240,512]{1,0:T(8,128)(2,1)S(1)} %get-tuple-element.56), channel_id=1, source_target_pairs={{0,130},{2,128},{128,2},{130,0},{1,131},{3,129},{129,3},{131,1},{4... | collective-permute-start | bytes 737288 | tf_op jit(solution)/shard_map/references/ppermute | solution.py:359
  9.2 1.1 %slice.3 = bf16[240,1024]{1,0:T(8,128)(2,1)S(1)} slice(bf16[240,4096]{1,0:T(8,128)(2,1)} %bitcast.22), slice={[0:240], [0:1024]} | slice | bytes 983040 | tf_op jit(solution)/shard_map/references/slice | solution.py:361
  10.3 1.3 %collective-permute-start.4 = (bf16[240,1024]{1,0:T(8,128)(2,1)S(1)}, bf16[240,1024]{1,0:T(8,128)(2,1)S(1)}, u32[]{:S(2)}, u32[]{:S(2)}) collective-permute-start(bf16[240,1024]{1,0:T(8,128)(2,1)S(1)} %slice.3), channel_id=1, source_target_pairs={{0,130},{2,128},{128,2},{130,0},{1,131},{3,129},{129,3},{131,1},{4... | collective-permute-start | bytes 1474568 | tf_op jit(solution)/shard_map/references/ppermute | solution.py:362
  11.6 4.0 %shift.2.own_ref = bf16[448,4096]{1,0:T(8,128)(2,1)S(1)} custom-call(f32[8,512]{1,0:T(8,128)S(1)} %pad.4.meta_ref.meta_a, bf16[448,4096]{1,0:T(8,128)(2,1)} %p_ref.1), custom_call_target="tpu_custom_call" | custom-call | flops 5000000000 | tf_op jit(solution)/shard_map/shift/pallas_call | solution.py:83
  15.6 1.5 %collective-permute-start.5 = (bf16[240,512]{1,0:T(8,128)(2,1)S(1)}, bf16[240,512]{1,0:T(8,128)(2,1)S(1)}, u32[]{:S(2)}, u32[]{:S(2)}) collective-permute-start(bf16[240,512]{1,0:T(8,128)(2,1)S(1)} %collective-permute-done.3.q0), channel_id=1, source_target_pairs={{32,0},{64,32},{96,64},{0,96},{33,1},{65,33},{97,65},{1,97},{34,2}... | collective-permute-start | bytes 737288 | tf_op jit(solution)/shard_map/references/ppermute | solution.py:325
  17.1 1.6 %collective-permute-start.6 = (bf16[240,512]{1,0:T(8,128)(2,1)S(1)}, bf16[240,512]{1,0:T(8,128)(2,1)S(1)}, u32[]{:S(2)}, u32[]{:S(2)}) collective-permute-start(bf16[240,512]{1,0:T(8,128)(2,1)S(1)} %collective-permute-done.3.q0), channel_id=1, source_target_pairs={{64,0},{96,32},{0,64},{32,96},{65,1},{97,33},{1,65},{33,97},{66,2}... | collective-permute-start | bytes 737288 | tf_op jit(solution)/shard_map/references/ppermute | solution.py:325
  18.7 1.9 %collective-permute-start.7 = (bf16[240,512]{1,0:T(8,128)(2,1)S(1)}, bf16[240,512]{1,0:T(8,128)(2,1)S(1)}, u32[]{:S(2)}, u32[]{:S(2)}) collective-permute-start(bf16[240,512]{1,0:T(8,128)(2,1)S(1)} %collective-permute-done.3.q0), channel_id=1, source_target_pairs={{96,0},{0,32},{32,64},{64,96},{97,1},{1,33},{33,65},{65,97},{98,2}... | collective-permute-start | bytes 737288 | tf_op jit(solution)/shard_map/references/ppermute | solution.py:325
  20.6 4.0 %shift.3.oth_ref = bf16[448,4096]{1,0:T(8,128)(2,1)S(1)} custom-call(f32[8,512]{1,0:T(8,128)S(1)} %collective-permute-done.meta_ref.meta_b, bf16[448,4096]{1,0:T(8,128)(2,1)} %collective-permute-done.2.p_ref), custom_call_target="tpu_custom_call" | custom-call | flops 5000000000 | tf_op jit(solution)/shard_map/shift/pallas_call | solution.py:83
  24.6 2.2 %collective-permute-start.8 = (bf16[240,512]{1,0:T(8,128)(2,1)S(1)}, bf16[240,512]{1,0:T(8,128)(2,1)S(1)}, u32[]{:S(2)}, u32[]{:S(2)}) collective-permute-start(bf16[240,512]{1,0:T(8,128)(2,1)S(1)} %collective-permute-done.1.z0), channel_id=1, source_target_pairs={{0,4},{4,0},{8,12},{12,8},{16,20},{20,16},{24,28},{28,24},{1,5},{5... | collective-permute-start | bytes 737288 | tf_op jit(solution)/shard_map/references/ppermute | solution.py:370
  26.8 4.6 %scores.2 = (bf16[1024,4096]{1,0:T(8,128)(2,1)S(1)}, f32[8,240,128]{2,1,0:T(8,128)S(1)}, f32[8,1024]{1,0:T(8,128)S(1)}, f32[8,240,128]{2,1,0:T(8,128)S(1)}, f32[240,128]{1,0:T(8,128)S(1)}) custom-call(s32[2]{0:T(128)S(1)} %pad_add_fusion.1.where_ref, bf16[448,4096]{1,0:T(8,128)(2,1)S(1)} %shift.2.own_ref, bf16[448,4096]{1,0:T(8,128)(2,1)S(1)} %shift.3.oth_ref, ...), custom_call_target="tpu_custom_call" | custom-call | flops 7000000000 | tf_op jit(solution)/shard_map/scores/pallas_call | solution.py:382
  31.4 3.0 %scores.3 = (f32[8,240,128]{2,1,0:T(8,128)S(1)}, f32[8,1024]{1,0:T(8,128)S(1)}) custom-call(s32[4]{0:T(128)S(1)} %pad_add_fusion.2.where_ref, bf16[1024,4096]{1,0:T(8,128)(2,1)S(1)} %get-tuple-element.66.w_ref, f32[1,4096]{1,0:T(1,128)S(1)} %maximum_divide_fusion.inv_ref, f32[240,1]{1,0:T(8,128)S(1)} %reshape_tile.9.bias_ref, ...), custom_call_target="tpu_custom_call" | custom-call | flops 5000000000 | tf_op jit(solution)/shard_map/scores/pallas_call | solution.py:391
  34.6 1.1 %collective-permute-done.9.theirs_ref = f32[8,1024]{1,0:T(8,128)S(1)} collective-permute-done((f32[8,1024]{1,0:T(8,128)S(1)}, f32[8,1024]{1,0:T(8,128)S(1)}, u32[]{:S(2)}, u32[]{:S(2)}) %collective-permute-start.9) | collective-permute-done | bytes 32800 | tf_op jit(solution)/shard_map/scores/ppermute | solution.py:403
  35.7 5.3 %sums.1 = (f32[4,8,64,128]{3,2,1,0:T(8,128)S(1)}, bf16[4,8,64,128]{3,2,1,0:T(8,128)(2,1)S(1)}, bf16[4,8,64,128]{3,2,1,0:T(8,128)(2,1)S(1)}, bf16[4,8,64,128]{3,2...) custom-call(s32[4]{0:T(128)S(1)} %pad_add_fusion.where_ref, ...), custom_call_target="tpu_custom_call" | custom-call | flops 6000000000 | tf_op jit(solution)/shard_map/sums/pallas_call | solution.py:406
  41.0 1.4 %collective-permute-start.10 = (bf16[4,8,64,128]{3,2,1,0:T(8,128)(2,1)S(1)}, bf16[4,8,64,128]{3,2,1,0:T(8,128)(2,1)S(1)}, u32[]{:S(2)}, u32[]{:S(2)}) collective-permute-start(bf16[4,8,64,128]{3,2,1,0:T(8,128)(2,1)S(1)} %get-tuple-element.75), channel_id=1, source_target_pairs={{0,2},{2,0},{128,130},{130,128},{1,3},{3,1},{129,131},{131,129},{4... | collective-permute-start | bytes 1572872 | tf_op jit(solution)/shard_map/reduce1/ppermute | solution.py:329
  42.4 1.2 %collective-permute-start.11 = (bf16[4,8,64,128]{3,2,1,0:T(8,128)(2,1)S(1)}, bf16[4,8,64,128]{3,2,1,0:T(8,128)(2,1)S(1)}, u32[]{:S(2)}, u32[]{:S(2)}) collective-permute-start(bf16[4,8,64,128]{3,2,1,0:T(8,128)(2,1)S(1)} %get-tuple-element.76), channel_id=1, source_target_pairs={{64,0},{96,32},{0,64},{32,96},{65,1},{97,33},{1,65},{33,97},{66,2}... | collective-permute-start | bytes 1572872 | tf_op jit(solution)/shard_map/reduce1/ppermute | solution.py:333
  43.6 1.1 %collective-permute-start.12 = (bf16[4,8,64,128]{3,2,1,0:T(8,128)(2,1)S(1)}, bf16[4,8,64,128]{3,2,1,0:T(8,128)(2,1)S(1)}, u32[]{:S(2)}, u32[]{:S(2)}) collective-permute-start(bf16[4,8,64,128]{3,2,1,0:T(8,128)(2,1)S(1)} %get-tuple-element.77), channel_id=1, source_target_pairs={{0,130},{2,128},{128,2},{130,0},{1,131},{3,129},{129,3},{131,1},{4... | collective-permute-start | bytes 1572872 | tf_op jit(solution)/shard_map/reduce1/ppermute | solution.py:329
  44.7 1.1 %collective-permute-start.13 = (bf16[4,8,64,128]{3,2,1,0:T(8,128)(2,1)S(1)}, bf16[4,8,64,128]{3,2,1,0:T(8,128)(2,1)S(1)}, u32[]{:S(2)}, u32[]{:S(2)}) collective-permute-start(bf16[4,8,64,128]{3,2,1,0:T(8,128)(2,1)S(1)} %get-tuple-element.78), channel_id=1, source_target_pairs={{32,0},{64,32},{96,64},{0,96},{33,1},{65,33},{97,65},{1,97},{34,2}... | collective-permute-start | bytes 1572872 | tf_op jit(solution)/shard_map/reduce1/ppermute | solution.py:333
  45.9 1.4 %collective-permute-start.14 = (bf16[4,8,64,128]{3,2,1,0:T(8,128)(2,1)S(1)}, bf16[4,8,64,128]{3,2,1,0:T(8,128)(2,1)S(1)}, u32[]{:S(2)}, u32[]{:S(2)}) collective-permute-start(bf16[4,8,64,128]{3,2,1,0:T(8,128)(2,1)S(1)} %get-tuple-element.79), channel_id=1, source_target_pairs={{0,128},{2,130},{128,0},{130,2},{1,129},{3,131},{129,1},{131,3},{4... | collective-permute-start | bytes 1572872 | tf_op jit(solution)/shard_map/reduce1/ppermute | solution.py:329
  47.3 10.1 %collective-permute-done.10.refs_2_ = bf16[4,8,64,128]{3,2,1,0:T(8,128)(2,1)S(1)} collective-permute-done((bf16[4,8,64,128]{3,2,1,0:T(8,128)(2,1)S(1)}, bf16[4,8,64,128]{3,2,1,0:T(8,128)(2,1)S(1)}, u32[]{:S(2)}, u32[]{:S(2)}) %collective-permute-start.10) | collective-permute-done | bytes 524320 | tf_op jit(solution)/shard_map/reduce1/ppermute | solution.py:329
  57.4 0.6 collective-permute-start.15
  58.1 0.7 collective-permute-done.11.refs_3_
  58.7 9.1 %collective-permute-done.12.refs_4_ = bf16[4,8,64,128]{3,2,1,0:T(8,128)(2,1)S(1)} collective-permute-done((bf16[4,8,64,128]{3,2,1,0:T(8,128)(2,1)S(1)}, bf16[4,8,64,128]{3,2,1,0:T(8,128)(2,1)S(1)}, u32[]{:S(2)}, u32[]{:S(2)}) %collective-permute-start.12) | collective-permute-done | bytes 524320 | tf_op jit(solution)/shard_map/reduce1/ppermute | solution.py:329
  67.8 1.0 collective-permute-done.13.refs_5_
  68.8 1.0 collective-permute-done.15.refs_7_
  70.3 1.3 %collective-permute-start.16 = (bf16[8,64,128]{2,1,0:T(8,128)(2,1)S(1)}, bf16[8,64,128]{2,1,0:T(8,128)(2,1)S(1)}, u32[]{:S(2)}, u32[]{:S(2)}) collective-permute-start(bf16[8,64,128]{2,1,0:T(8,128)(2,1)S(1)} %get-tuple-element.83), channel_id=1, source_target_pairs={{64,0},{96,32},{0,64},{32,96},{65,1},{97,33},{1,65},{33,97},{66,2}... | collective-permute-start | bytes 393224 | tf_op jit(solution)/shard_map/reduce2/ppermute | solution.py:333
  71.6 1.3 %collective-permute-start.17 = (bf16[8,64,128]{2,1,0:T(8,128)(2,1)S(1)}, bf16[8,64,128]{2,1,0:T(8,128)(2,1)S(1)}, u32[]{:S(2)}, u32[]{:S(2)}) collective-permute-start(bf16[8,64,128]{2,1,0:T(8,128)(2,1)S(1)} %get-tuple-element.84), channel_id=1, source_target_pairs={{0,2},{2,0},{128,130},{130,128},{1,3},{3,1},{129,131},{131,129},{4... | collective-permute-start | bytes 393224 | tf_op jit(solution)/shard_map/reduce2/ppermute | solution.py:329
  72.9 1.5 %collective-permute-start.18 = (bf16[8,64,128]{2,1,0:T(8,128)(2,1)S(1)}, bf16[8,64,128]{2,1,0:T(8,128)(2,1)S(1)}, u32[]{:S(2)}, u32[]{:S(2)}) collective-permute-start(bf16[8,64,128]{2,1,0:T(8,128)(2,1)S(1)} %get-tuple-element.85), channel_id=1, source_target_pairs={{32,0},{64,32},{96,64},{0,96},{33,1},{65,33},{97,65},{1,97},{34,2}... | collective-permute-start | bytes 393224 | tf_op jit(solution)/shard_map/reduce2/ppermute | solution.py:333
  74.4 2.2 %collective-permute-start.19 = (bf16[8,64,128]{2,1,0:T(8,128)(2,1)S(1)}, bf16[8,64,128]{2,1,0:T(8,128)(2,1)S(1)}, u32[]{:S(2)}, u32[]{:S(2)}) collective-permute-start(bf16[8,64,128]{2,1,0:T(8,128)(2,1)S(1)} %get-tuple-element.86), channel_id=1, source_target_pairs={{0,130},{2,128},{128,2},{130,0},{1,131},{3,129},{129,3},{131,1},{4... | collective-permute-start | bytes 393224 | tf_op jit(solution)/shard_map/reduce2/ppermute | solution.py:329
  77.2 1.0 collective-permute-done.16.refs_2_
  78.2 1.0 collective-permute-done.18.refs_4_
  79.2 1.4 %collective-permute-done.19.refs_5_ = bf16[8,64,128]{2,1,0:T(8,128)(2,1)S(1)} collective-permute-done((bf16[8,64,128]{2,1,0:T(8,128)(2,1)S(1)}, bf16[8,64,128]{2,1,0:T(8,128)(2,1)S(1)}, u32[]{:S(2)}, u32[]{:S(2)}) %collective-permute-start.19) | collective-permute-done | bytes 131104 | tf_op jit(solution)/shard_map/reduce2/ppermute | solution.py:329
  80.6 1.0 collective-permute-done.20.refs_6_
  81.5 1.6 %collective-permute-done.21.refs_7_ = bf16[8,64,128]{2,1,0:T(8,128)(2,1)S(1)} collective-permute-done((bf16[8,64,128]{2,1,0:T(8,128)(2,1)S(1)}, bf16[8,64,128]{2,1,0:T(8,128)(2,1)S(1)}, u32[]{:S(2)}, u32[]{:S(2)}) %collective-permute-start.21) | collective-permute-done | bytes 131104 | tf_op jit(solution)/shard_map/reduce2/ppermute | solution.py:329
  83.3 7.0 %collective-permute-start.22 = (f32[128,128]{1,0:T(8,128)S(1)}, f32[128,128]{1,0:T(8,128)S(1)}, u32[]{:S(2)}, u32[]{:S(2)}) collective-permute-start(f32[128,128]{1,0:T(8,128)S(1)} %get-tuple-element.90), channel_id=1, source_target_pairs={{16,0},{20,4},{24,8},{28,12},{0,16},{4,20},{8,24},{12,28},{17,1},{... | collective-permute-start | bytes 196616 | tf_op jit(solution)/shard_map/reduce3/ppermute | solution.py:337
  90.3 1.9 %collective-permute-start.23 = (f32[128,128]{1,0:T(8,128)S(1)}, f32[128,128]{1,0:T(8,128)S(1)}, u32[]{:S(2)}, u32[]{:S(2)}) collective-permute-start(f32[128,128]{1,0:T(8,128)S(1)} %get-tuple-element.91), channel_id=1, source_target_pairs={{20,0},{24,4},{28,8},{0,12},{4,16},{8,20},{12,24},{16,28},{21,1},{... | collective-permute-start | bytes 196616 | tf_op jit(solution)/shard_map/reduce3/ppermute | solution.py:337
  92.2 3.1 %collective-permute-start.24 = (f32[128,128]{1,0:T(8,128)S(1)}, f32[128,128]{1,0:T(8,128)S(1)}, u32[]{:S(2)}, u32[]{:S(2)}) collective-permute-start(f32[128,128]{1,0:T(8,128)S(1)} %get-tuple-element.92), channel_id=1, source_target_pairs={{12,0},{16,4},{20,8},{24,12},{28,16},{0,20},{4,24},{8,28},{13,1},{... | collective-permute-start | bytes 196616 | tf_op jit(solution)/shard_map/reduce3/ppermute | solution.py:337
  95.3 1.5 %collective-permute-start.25 = (f32[128,128]{1,0:T(8,128)S(1)}, f32[128,128]{1,0:T(8,128)S(1)}, u32[]{:S(2)}, u32[]{:S(2)}) collective-permute-start(f32[128,128]{1,0:T(8,128)S(1)} %get-tuple-element.93), channel_id=1, source_target_pairs={{24,0},{28,4},{0,8},{4,12},{8,16},{12,20},{16,24},{20,28},{25,1},{... | collective-permute-start | bytes 196616 | tf_op jit(solution)/shard_map/reduce3/ppermute | solution.py:337
  96.8 2.7 %collective-permute-start.26 = (f32[128,128]{1,0:T(8,128)S(1)}, f32[128,128]{1,0:T(8,128)S(1)}, u32[]{:S(2)}, u32[]{:S(2)}) collective-permute-start(f32[128,128]{1,0:T(8,128)S(1)} %get-tuple-element.94), channel_id=1, source_target_pairs={{8,0},{12,4},{16,8},{20,12},{24,16},{28,20},{0,24},{4,28},{9,1},{1... | collective-permute-start | bytes 196616 | tf_op jit(solution)/shard_map/reduce3/ppermute | solution.py:337
  99.5 1.0 collective-permute-start.27
  100.5 2.2 %collective-permute-start.28 = (f32[128,128]{1,0:T(8,128)S(1)}, f32[128,128]{1,0:T(8,128)S(1)}, u32[]{:S(2)}, u32[]{:S(2)}) collective-permute-start(f32[128,128]{1,0:T(8,128)S(1)} %get-tuple-element.96), channel_id=1, source_target_pairs={{4,0},{8,4},{12,8},{16,12},{20,16},{24,20},{28,24},{0,28},{5,1},{9... | collective-permute-start | bytes 196616 | tf_op jit(solution)/shard_map/reduce3/ppermute | solution.py:337
  102.7 2.2 %collective-permute-done.27.refs_6_ = f32[128,128]{1,0:T(8,128)S(1)} collective-permute-done((f32[128,128]{1,0:T(8,128)S(1)}, f32[128,128]{1,0:T(8,128)S(1)}, u32[]{:S(2)}, u32[]{:S(2)}) %collective-permute-start.27) | collective-permute-done | bytes 65568 | tf_op jit(solution)/shard_map/reduce3/ppermute | solution.py:337
  104.9 0.8 means.1
  (37 shorter events, 1.9 us)
Async XLA Ops:
  0.0 15.6 %collective-permute-start.2 = (bf16[448,4096]{1,0:T(8,128)(2,1)}, bf16[448,4096]{1,0:T(8,128)(2,1)}, u32[]{:S(2)}, u32[]{:S(2)}) collective-permute-start(bf16[448,4096]{1,0:T(8,128)(2,1)} %p_ref.1), channel_id=1, source_target_pairs={{0,1},{1,0},{2,3},{3,2},{4,5},{5,4},{6,7},{7,6},{8,9},{9,8},{10,11... | collective-permute-start | bytes 11010056 | tf_op jit(solution)/shard_map/swap/ppermute | solution.py:347
  1.8 5.3 %collective-permute-start = (f32[8,512]{1,0:T(8,128)S(1)}, f32[8,512]{1,0:T(8,128)S(1)}, u32[]{:S(2)}, u32[]{:S(2)}) collective-permute-start(f32[8,512]{1,0:T(8,128)S(1)} %pad.4.meta_ref.meta_a), channel_id=1, source_target_pairs={{0,1},{1,0},{2,3},{3,2},{4,5},{5,4},{6,7},{7,6},{8,9},{9,8},{10,11... | collective-permute-start | bytes 49160 | tf_op jit(solution)/shard_map/swap/ppermute | solution.py:356
  2.4 13.2 %collective-permute-start.3 = (bf16[240,512]{1,0:T(8,128)(2,1)S(1)}, bf16[240,512]{1,0:T(8,128)(2,1)S(1)}, u32[]{:S(2)}, u32[]{:S(2)}) collective-permute-start(bf16[240,512]{1,0:T(8,128)(2,1)S(1)} %get-tuple-element.60), channel_id=1, source_target_pairs={{0,130},{2,128},{128,2},{130,0},{1,131},{3,129},{129,3},{131,1},{4... | collective-permute-start | bytes 737288 | tf_op jit(solution)/shard_map/references/ppermute | solution.py:352
  7.1 17.5 %collective-permute-start.1 = (bf16[240,512]{1,0:T(8,128)(2,1)S(1)}, bf16[240,512]{1,0:T(8,128)(2,1)S(1)}, u32[]{:S(2)}, u32[]{:S(2)}) collective-permute-start(bf16[240,512]{1,0:T(8,128)(2,1)S(1)} %get-tuple-element.56), channel_id=1, source_target_pairs={{0,130},{2,128},{128,2},{130,0},{1,131},{3,129},{129,3},{131,1},{4... | collective-permute-start | bytes 737288 | tf_op jit(solution)/shard_map/references/ppermute | solution.py:359
  10.3 21.1 %collective-permute-start.4 = (bf16[240,1024]{1,0:T(8,128)(2,1)S(1)}, bf16[240,1024]{1,0:T(8,128)(2,1)S(1)}, u32[]{:S(2)}, u32[]{:S(2)}) collective-permute-start(bf16[240,1024]{1,0:T(8,128)(2,1)S(1)} %slice.3), channel_id=1, source_target_pairs={{0,130},{2,128},{128,2},{130,0},{1,131},{3,129},{129,3},{131,1},{4... | collective-permute-start | bytes 1474568 | tf_op jit(solution)/shard_map/references/ppermute | solution.py:362
  15.6 11.2 %copy-start = (bf16[8,30,4096]{2,0,1:T(8,128)(2,1)S(1)}, bf16[8,30,4096]{2,0,1:T(8,128)(2,1)}, u32[]{:S(2)}) copy-start(bf16[8,30,4096]{2,0,1:T(8,128)(2,1)} %param.9) | copy-start | bytes 5898244
  15.6 15.8 %collective-permute-start.5 = (bf16[240,512]{1,0:T(8,128)(2,1)S(1)}, bf16[240,512]{1,0:T(8,128)(2,1)S(1)}, u32[]{:S(2)}, u32[]{:S(2)}) collective-permute-start(bf16[240,512]{1,0:T(8,128)(2,1)S(1)} %collective-permute-done.3.q0), channel_id=1, source_target_pairs={{32,0},{64,32},{96,64},{0,96},{33,1},{65,33},{97,65},{1,97},{34,2}... | collective-permute-start | bytes 737288 | tf_op jit(solution)/shard_map/references/ppermute | solution.py:325
  17.1 14.3 %collective-permute-start.6 = (bf16[240,512]{1,0:T(8,128)(2,1)S(1)}, bf16[240,512]{1,0:T(8,128)(2,1)S(1)}, u32[]{:S(2)}, u32[]{:S(2)}) collective-permute-start(bf16[240,512]{1,0:T(8,128)(2,1)S(1)} %collective-permute-done.3.q0), channel_id=1, source_target_pairs={{64,0},{96,32},{0,64},{32,96},{65,1},{97,33},{1,65},{33,97},{66,2}... | collective-permute-start | bytes 737288 | tf_op jit(solution)/shard_map/references/ppermute | solution.py:325
  18.7 12.7 %collective-permute-start.7 = (bf16[240,512]{1,0:T(8,128)(2,1)S(1)}, bf16[240,512]{1,0:T(8,128)(2,1)S(1)}, u32[]{:S(2)}, u32[]{:S(2)}) collective-permute-start(bf16[240,512]{1,0:T(8,128)(2,1)S(1)} %collective-permute-done.3.q0), channel_id=1, source_target_pairs={{96,0},{0,32},{32,64},{64,96},{97,1},{1,33},{33,65},{65,97},{98,2}... | collective-permute-start | bytes 737288 | tf_op jit(solution)/shard_map/references/ppermute | solution.py:325
  24.6 6.8 %collective-permute-start.8 = (bf16[240,512]{1,0:T(8,128)(2,1)S(1)}, bf16[240,512]{1,0:T(8,128)(2,1)S(1)}, u32[]{:S(2)}, u32[]{:S(2)}) collective-permute-start(bf16[240,512]{1,0:T(8,128)(2,1)S(1)} %collective-permute-done.1.z0), channel_id=1, source_target_pairs={{0,4},{4,0},{8,12},{12,8},{16,20},{20,16},{24,28},{28,24},{1,5},{5... | collective-permute-start | bytes 737288 | tf_op jit(solution)/shard_map/references/ppermute | solution.py:370
  34.4 1.3 %collective-permute-start.9 = (f32[8,1024]{1,0:T(8,128)S(1)}, f32[8,1024]{1,0:T(8,128)S(1)}, u32[]{:S(2)}, u32[]{:S(2)}) collective-permute-start(f32[8,1024]{1,0:T(8,128)S(1)} %get-tuple-element.72.mine_ref), channel_id=1, source_target_pairs={{0,1},{1,0},{2,3},{3,2},{4,5},{5,4},{6,7},{7,6},{8,9},{9,8},{10,11... | collective-permute-start | bytes 98312 | tf_op jit(solution)/shard_map/scores/ppermute | solution.py:403
  41.0 63.9 %copy-start.1 = (f32[2048]{0:T(1024)S(1)}, f32[2048]{0:T(1024)}, u32[]{:S(2)}) copy-start(f32[2048]{0:T(1024)} %param.11) | copy-start | bytes 24580
  41.0 16.4 %collective-permute-start.10 = (bf16[4,8,64,128]{3,2,1,0:T(8,128)(2,1)S(1)}, bf16[4,8,64,128]{3,2,1,0:T(8,128)(2,1)S(1)}, u32[]{:S(2)}, u32[]{:S(2)}) collective-permute-start(bf16[4,8,64,128]{3,2,1,0:T(8,128)(2,1)S(1)} %get-tuple-element.75), channel_id=1, source_target_pairs={{0,2},{2,0},{128,130},{130,128},{1,3},{3,1},{129,131},{131,129},{4... | collective-permute-start | bytes 1572872 | tf_op jit(solution)/shard_map/reduce1/ppermute | solution.py:329
  42.4 16.4 %collective-permute-start.11 = (bf16[4,8,64,128]{3,2,1,0:T(8,128)(2,1)S(1)}, bf16[4,8,64,128]{3,2,1,0:T(8,128)(2,1)S(1)}, u32[]{:S(2)}, u32[]{:S(2)}) collective-permute-start(bf16[4,8,64,128]{3,2,1,0:T(8,128)(2,1)S(1)} %get-tuple-element.76), channel_id=1, source_target_pairs={{64,0},{96,32},{0,64},{32,96},{65,1},{97,33},{1,65},{33,97},{66,2}... | collective-permute-start | bytes 1572872 | tf_op jit(solution)/shard_map/reduce1/ppermute | solution.py:333
  43.6 24.2 %collective-permute-start.12 = (bf16[4,8,64,128]{3,2,1,0:T(8,128)(2,1)S(1)}, bf16[4,8,64,128]{3,2,1,0:T(8,128)(2,1)S(1)}, u32[]{:S(2)}, u32[]{:S(2)}) collective-permute-start(bf16[4,8,64,128]{3,2,1,0:T(8,128)(2,1)S(1)} %get-tuple-element.77), channel_id=1, source_target_pairs={{0,130},{2,128},{128,2},{130,0},{1,131},{3,129},{129,3},{131,1},{4... | collective-permute-start | bytes 1572872 | tf_op jit(solution)/shard_map/reduce1/ppermute | solution.py:329
  44.7 24.1 %collective-permute-start.13 = (bf16[4,8,64,128]{3,2,1,0:T(8,128)(2,1)S(1)}, bf16[4,8,64,128]{3,2,1,0:T(8,128)(2,1)S(1)}, u32[]{:S(2)}, u32[]{:S(2)}) collective-permute-start(bf16[4,8,64,128]{3,2,1,0:T(8,128)(2,1)S(1)} %get-tuple-element.78), channel_id=1, source_target_pairs={{32,0},{64,32},{96,64},{0,96},{33,1},{65,33},{97,65},{1,97},{34,2}... | collective-permute-start | bytes 1572872 | tf_op jit(solution)/shard_map/reduce1/ppermute | solution.py:333
  45.9 23.0 %collective-permute-start.14 = (bf16[4,8,64,128]{3,2,1,0:T(8,128)(2,1)S(1)}, bf16[4,8,64,128]{3,2,1,0:T(8,128)(2,1)S(1)}, u32[]{:S(2)}, u32[]{:S(2)}) collective-permute-start(bf16[4,8,64,128]{3,2,1,0:T(8,128)(2,1)S(1)} %get-tuple-element.79), channel_id=1, source_target_pairs={{0,128},{2,130},{128,0},{130,2},{1,129},{3,131},{129,1},{131,3},{4... | collective-permute-start | bytes 1572872 | tf_op jit(solution)/shard_map/reduce1/ppermute | solution.py:329
  57.4 12.4 %collective-permute-start.15 = (bf16[4,8,64,128]{3,2,1,0:T(8,128)(2,1)S(1)}, bf16[4,8,64,128]{3,2,1,0:T(8,128)(2,1)S(1)}, u32[]{:S(2)}, u32[]{:S(2)}) collective-permute-start(bf16[4,8,64,128]{3,2,1,0:T(8,128)(2,1)S(1)} %get-tuple-element.80), channel_id=1, source_target_pairs={{96,0},{0,32},{32,64},{64,96},{97,1},{1,33},{33,65},{65,97},{98,2}... | collective-permute-start | bytes 1572872 | tf_op jit(solution)/shard_map/reduce1/ppermute | solution.py:333
  70.3 7.9 %collective-permute-start.16 = (bf16[8,64,128]{2,1,0:T(8,128)(2,1)S(1)}, bf16[8,64,128]{2,1,0:T(8,128)(2,1)S(1)}, u32[]{:S(2)}, u32[]{:S(2)}) collective-permute-start(bf16[8,64,128]{2,1,0:T(8,128)(2,1)S(1)} %get-tuple-element.83), channel_id=1, source_target_pairs={{64,0},{96,32},{0,64},{32,96},{65,1},{97,33},{1,65},{33,97},{66,2}... | collective-permute-start | bytes 393224 | tf_op jit(solution)/shard_map/reduce2/ppermute | solution.py:333
  71.6 6.6 %collective-permute-start.17 = (bf16[8,64,128]{2,1,0:T(8,128)(2,1)S(1)}, bf16[8,64,128]{2,1,0:T(8,128)(2,1)S(1)}, u32[]{:S(2)}, u32[]{:S(2)}) collective-permute-start(bf16[8,64,128]{2,1,0:T(8,128)(2,1)S(1)} %get-tuple-element.84), channel_id=1, source_target_pairs={{0,2},{2,0},{128,130},{130,128},{1,3},{3,1},{129,131},{131,129},{4... | collective-permute-start | bytes 393224 | tf_op jit(solution)/shard_map/reduce2/ppermute | solution.py:329
  72.9 6.3 %collective-permute-start.18 = (bf16[8,64,128]{2,1,0:T(8,128)(2,1)S(1)}, bf16[8,64,128]{2,1,0:T(8,128)(2,1)S(1)}, u32[]{:S(2)}, u32[]{:S(2)}) collective-permute-start(bf16[8,64,128]{2,1,0:T(8,128)(2,1)S(1)} %get-tuple-element.85), channel_id=1, source_target_pairs={{32,0},{64,32},{96,64},{0,96},{33,1},{65,33},{97,65},{1,97},{34,2}... | collective-permute-start | bytes 393224 | tf_op jit(solution)/shard_map/reduce2/ppermute | solution.py:333
  74.4 6.2 %collective-permute-start.19 = (bf16[8,64,128]{2,1,0:T(8,128)(2,1)S(1)}, bf16[8,64,128]{2,1,0:T(8,128)(2,1)S(1)}, u32[]{:S(2)}, u32[]{:S(2)}) collective-permute-start(bf16[8,64,128]{2,1,0:T(8,128)(2,1)S(1)} %get-tuple-element.86), channel_id=1, source_target_pairs={{0,130},{2,128},{128,2},{130,0},{1,131},{3,129},{129,3},{131,1},{4... | collective-permute-start | bytes 393224 | tf_op jit(solution)/shard_map/reduce2/ppermute | solution.py:329
  76.6 5.0 %collective-permute-start.20 = (bf16[8,64,128]{2,1,0:T(8,128)(2,1)S(1)}, bf16[8,64,128]{2,1,0:T(8,128)(2,1)S(1)}, u32[]{:S(2)}, u32[]{:S(2)}) collective-permute-start(bf16[8,64,128]{2,1,0:T(8,128)(2,1)S(1)} %get-tuple-element.87), channel_id=1, source_target_pairs={{96,0},{0,32},{32,64},{64,96},{97,1},{1,33},{33,65},{65,97},{98,2}... | collective-permute-start | bytes 393224 | tf_op jit(solution)/shard_map/reduce2/ppermute | solution.py:333
  78.2 5.0 %collective-permute-start.21 = (bf16[8,64,128]{2,1,0:T(8,128)(2,1)S(1)}, bf16[8,64,128]{2,1,0:T(8,128)(2,1)S(1)}, u32[]{:S(2)}, u32[]{:S(2)}) collective-permute-start(bf16[8,64,128]{2,1,0:T(8,128)(2,1)S(1)} %get-tuple-element.88), channel_id=1, source_target_pairs={{0,128},{2,130},{128,0},{130,2},{1,129},{3,131},{129,1},{131,3},{4... | collective-permute-start | bytes 393224 | tf_op jit(solution)/shard_map/reduce2/ppermute | solution.py:329
  83.3 16.2 %collective-permute-start.22 = (f32[128,128]{1,0:T(8,128)S(1)}, f32[128,128]{1,0:T(8,128)S(1)}, u32[]{:S(2)}, u32[]{:S(2)}) collective-permute-start(f32[128,128]{1,0:T(8,128)S(1)} %get-tuple-element.90), channel_id=1, source_target_pairs={{16,0},{20,4},{24,8},{28,12},{0,16},{4,20},{8,24},{12,28},{17,1},{... | collective-permute-start | bytes 196616 | tf_op jit(solution)/shard_map/reduce3/ppermute | solution.py:337
  90.3 10.2 %collective-permute-start.23 = (f32[128,128]{1,0:T(8,128)S(1)}, f32[128,128]{1,0:T(8,128)S(1)}, u32[]{:S(2)}, u32[]{:S(2)}) collective-permute-start(f32[128,128]{1,0:T(8,128)S(1)} %get-tuple-element.91), channel_id=1, source_target_pairs={{20,0},{24,4},{28,8},{0,12},{4,16},{8,20},{12,24},{16,28},{21,1},{... | collective-permute-start | bytes 196616 | tf_op jit(solution)/shard_map/reduce3/ppermute | solution.py:337
  92.2 10.5 %collective-permute-start.24 = (f32[128,128]{1,0:T(8,128)S(1)}, f32[128,128]{1,0:T(8,128)S(1)}, u32[]{:S(2)}, u32[]{:S(2)}) collective-permute-start(f32[128,128]{1,0:T(8,128)S(1)} %get-tuple-element.92), channel_id=1, source_target_pairs={{12,0},{16,4},{20,8},{24,12},{28,16},{0,20},{4,24},{8,28},{13,1},{... | collective-permute-start | bytes 196616 | tf_op jit(solution)/shard_map/reduce3/ppermute | solution.py:337
  95.3 7.4 %collective-permute-start.25 = (f32[128,128]{1,0:T(8,128)S(1)}, f32[128,128]{1,0:T(8,128)S(1)}, u32[]{:S(2)}, u32[]{:S(2)}) collective-permute-start(f32[128,128]{1,0:T(8,128)S(1)} %get-tuple-element.93), channel_id=1, source_target_pairs={{24,0},{28,4},{0,8},{4,12},{8,16},{12,20},{16,24},{20,28},{25,1},{... | collective-permute-start | bytes 196616 | tf_op jit(solution)/shard_map/reduce3/ppermute | solution.py:337
  96.8 5.9 %collective-permute-start.26 = (f32[128,128]{1,0:T(8,128)S(1)}, f32[128,128]{1,0:T(8,128)S(1)}, u32[]{:S(2)}, u32[]{:S(2)}) collective-permute-start(f32[128,128]{1,0:T(8,128)S(1)} %get-tuple-element.94), channel_id=1, source_target_pairs={{8,0},{12,4},{16,8},{20,12},{24,16},{28,20},{0,24},{4,28},{9,1},{1... | collective-permute-start | bytes 196616 | tf_op jit(solution)/shard_map/reduce3/ppermute | solution.py:337
  99.5 5.5 %collective-permute-start.27 = (f32[128,128]{1,0:T(8,128)S(1)}, f32[128,128]{1,0:T(8,128)S(1)}, u32[]{:S(2)}, u32[]{:S(2)}) collective-permute-start(f32[128,128]{1,0:T(8,128)S(1)} %get-tuple-element.95), channel_id=1, source_target_pairs={{28,0},{0,4},{4,8},{8,12},{12,16},{16,20},{20,24},{24,28},{29,1},{... | collective-permute-start | bytes 196616 | tf_op jit(solution)/shard_map/reduce3/ppermute | solution.py:337
  100.5 4.5 %collective-permute-start.28 = (f32[128,128]{1,0:T(8,128)S(1)}, f32[128,128]{1,0:T(8,128)S(1)}, u32[]{:S(2)}, u32[]{:S(2)}) collective-permute-start(f32[128,128]{1,0:T(8,128)S(1)} %get-tuple-element.96), channel_id=1, source_target_pairs={{4,0},{8,4},{12,8},{16,12},{20,16},{24,20},{28,24},{0,28},{5,1},{9... | collective-permute-start | bytes 196616 | tf_op jit(solution)/shard_map/reduce3/ppermute | solution.py:337

commit v2 on v1

--- a/solution.py
+++ b/solution.py
@@ -361,8 +361,8 @@
         direct, meta_oth = lax.optimization_barrier((later_refs[:, :DIRECT], meta_oth))
         direct = lax.ppermute(direct, X, X_SWAP)
     with jax.named_scope("shift"):
+        raw, crossed, meta = lax.optimization_barrier((raw, crossed, meta))
         own = shift_particles(particles, meta, 48)
-        raw, crossed = lax.optimization_barrier((raw, crossed))
         oth = shift_particles(raw, meta_oth, 12)
     with jax.named_scope("references"):
         quarters = [from_y(crossed, s) for s in (1, 2, 3)]

time: 108 us -> 106 us (0.981); the launches traced: 106 us -> 106 us
  transfers between devices with their start and end apart: 29 -> 29, of which waited for: 12 -> 13; matrix products, arithmetic and copies ran while one was open for 5% -> 5% of each run, Pallas kernels for 12% -> 12%
where the time goes in v2:
time: 106 us
  starting transfers between devices  47.3 us (45%)
  waiting for transfers between devices  31.4 us (30%)
  Pallas kernels  22.3 us (21%)
  local copies, waits for them, and re-layouts  3.12 us (3%)
  other arithmetic  1.75 us (2%)
    ppermute x6, waiting for transfers between devices, to_x(): lax.ppermute(value, X, [(i, i ^ flips >> 1 ^ (flips & 1) << 1) for i in r...  22.5 us
    ppermute x7, starting transfers between devices, to_z(): return lax.ppermute(value, 'z', ring(8, -step))  19.5 us
    pallas_call x2, Pallas kernels, shift_particles(): pl.pallas_call(shift_kernel, out_shape=jax.ShapeDtypeStruct((NP, WIDE), B...  8.08 us
    ppermute x6, starting transfers between devices, to_x(): lax.ppermute(value, X, [(i, i ^ flips >> 1 ^ (flips & 1) << 1) for i in r...  7.8 us
    ppermute x6, starting transfers between devices, to_y(): return lax.ppermute(value, 'y', ring(4, -step))  6.25 us
    pallas_call x1, Pallas kernels, local(): pl.pallas_call(sums_kernel, out_shape=([jax.ShapeDtypeStruct((4, 8, PROWS...  5.32 us
    ppermute x6, waiting for transfers between devices, to_y(): return lax.ppermute(value, 'y', ring(4, -step))  5.11 us
    ppermute x3, starting transfers between devices, from_y(): return lax.ppermute(value, 'y', ring(4, step))  4.93 us
  transfers between devices with their start and end apart: 29, of which 13 were waited for; matrix products, arithmetic and copies ran while one was open for 5% of the time, Pallas kernels for 12%

profile of v2, /device:TPU:8, one launch (start us, length us, event | category | flops | bytes accessed | tf_op | source)
XLA Modules:
  0.0 106.1 jit_solution(10750587342243751093)
XLA Ops:
  0.0 1.1 %constant_dynamic-slice_fusion.2 = (bf16[240,512]{1,0:T(8,128)(2,1)S(1)}, bf16[240,512]{1,0:T(8,128)(2,1)S(1)}) fusion(bf16[240,4096]{1,0:T(8,128)(2,1)} %bitcast.21, s32[]{:T(128)S(6)} %select_n.17, s32[]{:T(128)S(6)} %select_n.16), kind=kLoop, calls=%fused_computation.4 | loop fusion | bytes 983048 | tf_op jit(solution)/shard_map/references/dynamic_slice | solution.py:350
  1.1 2.8 %collective-permute-start.1 = (bf16[240,512]{1,0:T(8,128)(2,1)S(1)}, bf16[240,512]{1,0:T(8,128)(2,1)S(1)}, u32[]{:S(2)}, u32[]{:S(2)}) collective-permute-start(bf16[240,512]{1,0:T(8,128)(2,1)S(1)} %get-tuple-element.52), channel_id=1, source_target_pairs={{0,130},{2,128},{128,2},{130,0},{1,131},{3,129},{129,3},{131,1},{4... | collective-permute-start | bytes 737288 | tf_op jit(solution)/shard_map/references/ppermute | solution.py:352
  3.9 0.7 add_convert_fusion
  5.0 0.8 maximum_divide_fusion.inv_ref
  5.9 0.7 log.3
  6.9 2.3 %collective-permute-start.3 = (bf16[240,512]{1,0:T(8,128)(2,1)S(1)}, bf16[240,512]{1,0:T(8,128)(2,1)S(1)}, u32[]{:S(2)}, u32[]{:S(2)}) collective-permute-start(bf16[240,512]{1,0:T(8,128)(2,1)S(1)} %get-tuple-element.59), channel_id=1, source_target_pairs={{0,130},{2,128},{128,2},{130,0},{1,131},{3,129},{129,3},{131,1},{4... | collective-permute-start | bytes 737288 | tf_op jit(solution)/shard_map/references/ppermute | solution.py:359
  9.2 1.1 %slice.3 = bf16[240,1024]{1,0:T(8,128)(2,1)S(1)} slice(bf16[240,4096]{1,0:T(8,128)(2,1)} %bitcast.22), slice={[0:240], [0:1024]} | slice | bytes 983040 | tf_op jit(solution)/shard_map/references/slice | solution.py:361
  10.3 1.1 %collective-permute-start.4 = (bf16[240,1024]{1,0:T(8,128)(2,1)S(1)}, bf16[240,1024]{1,0:T(8,128)(2,1)S(1)}, u32[]{:S(2)}, u32[]{:S(2)}) collective-permute-start(bf16[240,1024]{1,0:T(8,128)(2,1)S(1)} %slice.3), channel_id=1, source_target_pairs={{0,130},{2,128},{128,2},{130,0},{1,131},{3,129},{129,3},{131,1},{4... | collective-permute-start | bytes 1474568 | tf_op jit(solution)/shard_map/references/ppermute | solution.py:362
  11.4 1.9 %collective-permute-start.5 = (bf16[240,512]{1,0:T(8,128)(2,1)S(1)}, bf16[240,512]{1,0:T(8,128)(2,1)S(1)}, u32[]{:S(2)}, u32[]{:S(2)}) collective-permute-start(bf16[240,512]{1,0:T(8,128)(2,1)S(1)} %collective-permute-done.1.q0), channel_id=1, source_target_pairs={{32,0},{64,32},{96,64},{0,96},{33,1},{65,33},{97,65},{1,97},{34,2}... | collective-permute-start | bytes 737288 | tf_op jit(solution)/shard_map/references/ppermute | solution.py:325
  13.3 1.1 %collective-permute-start.6 = (bf16[240,512]{1,0:T(8,128)(2,1)S(1)}, bf16[240,512]{1,0:T(8,128)(2,1)S(1)}, u32[]{:S(2)}, u32[]{:S(2)}) collective-permute-start(bf16[240,512]{1,0:T(8,128)(2,1)S(1)} %collective-permute-done.1.q0), channel_id=1, source_target_pairs={{64,0},{96,32},{0,64},{32,96},{65,1},{97,33},{1,65},{33,97},{66,2}... | collective-permute-start | bytes 737288 | tf_op jit(solution)/shard_map/references/ppermute | solution.py:325
  14.4 1.9 %collective-permute-start.7 = (bf16[240,512]{1,0:T(8,128)(2,1)S(1)}, bf16[240,512]{1,0:T(8,128)(2,1)S(1)}, u32[]{:S(2)}, u32[]{:S(2)}) collective-permute-start(bf16[240,512]{1,0:T(8,128)(2,1)S(1)} %collective-permute-done.1.q0), channel_id=1, source_target_pairs={{96,0},{0,32},{32,64},{64,96},{97,1},{1,33},{33,65},{65,97},{98,2}... | collective-permute-start | bytes 737288 | tf_op jit(solution)/shard_map/references/ppermute | solution.py:325
  16.3 4.0 %shift.2.own_ref = bf16[448,4096]{1,0:T(8,128)(2,1)S(1)} custom-call(f32[8,512]{1,0:T(8,128)S(1)} %pad.4.meta_ref.meta_a, bf16[448,4096]{1,0:T(8,128)(2,1)} %p_ref.1), custom_call_target="tpu_custom_call" | custom-call | flops 5000000000 | tf_op jit(solution)/shard_map/shift/pallas_call | solution.py:83
  20.3 4.1 %shift.3.oth_ref = bf16[448,4096]{1,0:T(8,128)(2,1)S(1)} custom-call(f32[8,512]{1,0:T(8,128)S(1)} %collective-permute-done.2.meta_ref.meta_b, bf16[448,4096]{1,0:T(8,128)(2,1)} %collective-permute-done.p_ref), custom_call_target="tpu_custom_call" | custom-call | flops 5000000000 | tf_op jit(solution)/shard_map/shift/pallas_call | solution.py:83
  24.5 2.2 %collective-permute-start.8 = (bf16[240,512]{1,0:T(8,128)(2,1)S(1)}, bf16[240,512]{1,0:T(8,128)(2,1)S(1)}, u32[]{:S(2)}, u32[]{:S(2)}) collective-permute-start(bf16[240,512]{1,0:T(8,128)(2,1)S(1)} %collective-permute-done.3.z0), channel_id=1, source_target_pairs={{0,4},{4,0},{8,12},{12,8},{16,20},{20,16},{24,28},{28,24},{1,5},{5... | collective-permute-start | bytes 737288 | tf_op jit(solution)/shard_map/references/ppermute | solution.py:370
  26.6 4.5 %scores.2 = (bf16[1024,4096]{1,0:T(8,128)(2,1)S(1)}, f32[8,240,128]{2,1,0:T(8,128)S(1)}, f32[8,1024]{1,0:T(8,128)S(1)}, f32[8,240,128]{2,1,0:T(8,128)S(1)}, f32[240,128]{1,0:T(8,128)S(1)}) custom-call(s32[2]{0:T(128)S(1)} %pad_add_fusion.1.where_ref, bf16[448,4096]{1,0:T(8,128)(2,1)S(1)} %shift.2.own_ref, bf16[448,4096]{1,0:T(8,128)(2,1)S(1)} %shift.3.oth_ref, ...), custom_call_target="tpu_custom_call" | custom-call | flops 7000000000 | tf_op jit(solution)/shard_map/scores/pallas_call | solution.py:382
  31.6 3.0 %scores.3 = (f32[8,240,128]{2,1,0:T(8,128)S(1)}, f32[8,1024]{1,0:T(8,128)S(1)}) custom-call(s32[4]{0:T(128)S(1)} %pad_add_fusion.2.where_ref, bf16[1024,4096]{1,0:T(8,128)(2,1)S(1)} %get-tuple-element.68.w_ref, f32[1,4096]{1,0:T(1,128)S(1)} %maximum_divide_fusion.inv_ref, f32[240,1]{1,0:T(8,128)S(1)} %reshape_tile.9.bias_ref, ...), custom_call_target="tpu_custom_call" | custom-call | flops 5000000000 | tf_op jit(solution)/shard_map/scores/pallas_call | solution.py:391
  34.8 1.1 %collective-permute-done.9.theirs_ref = f32[8,1024]{1,0:T(8,128)S(1)} collective-permute-done((f32[8,1024]{1,0:T(8,128)S(1)}, f32[8,1024]{1,0:T(8,128)S(1)}, u32[]{:S(2)}, u32[]{:S(2)}) %collective-permute-start.9) | collective-permute-done | bytes 32800 | tf_op jit(solution)/shard_map/scores/ppermute | solution.py:403
  35.9 5.3 %sums.1 = (f32[4,8,64,128]{3,2,1,0:T(8,128)S(1)}, bf16[4,8,64,128]{3,2,1,0:T(8,128)(2,1)S(1)}, bf16[4,8,64,128]{3,2,1,0:T(8,128)(2,1)S(1)}, bf16[4,8,64,128]{3,2...) custom-call(s32[4]{0:T(128)S(1)} %pad_add_fusion.where_ref, ...), custom_call_target="tpu_custom_call" | custom-call | flops 6000000000 | tf_op jit(solution)/shard_map/sums/pallas_call | solution.py:406
  41.2 1.3 %collective-permute-start.10 = (bf16[4,8,64,128]{3,2,1,0:T(8,128)(2,1)S(1)}, bf16[4,8,64,128]{3,2,1,0:T(8,128)(2,1)S(1)}, u32[]{:S(2)}, u32[]{:S(2)}) collective-permute-start(bf16[4,8,64,128]{3,2,1,0:T(8,128)(2,1)S(1)} %get-tuple-element.77), channel_id=1, source_target_pairs={{0,2},{2,0},{128,130},{130,128},{1,3},{3,1},{129,131},{131,129},{4... | collective-permute-start | bytes 1572872 | tf_op jit(solution)/shard_map/reduce1/ppermute | solution.py:329
  42.5 1.2 %collective-permute-start.11 = (bf16[4,8,64,128]{3,2,1,0:T(8,128)(2,1)S(1)}, bf16[4,8,64,128]{3,2,1,0:T(8,128)(2,1)S(1)}, u32[]{:S(2)}, u32[]{:S(2)}) collective-permute-start(bf16[4,8,64,128]{3,2,1,0:T(8,128)(2,1)S(1)} %get-tuple-element.78), channel_id=1, source_target_pairs={{64,0},{96,32},{0,64},{32,96},{65,1},{97,33},{1,65},{33,97},{66,2}... | collective-permute-start | bytes 1572872 | tf_op jit(solution)/shard_map/reduce1/ppermute | solution.py:333
  43.8 1.1 %collective-permute-start.12 = (bf16[4,8,64,128]{3,2,1,0:T(8,128)(2,1)S(1)}, bf16[4,8,64,128]{3,2,1,0:T(8,128)(2,1)S(1)}, u32[]{:S(2)}, u32[]{:S(2)}) collective-permute-start(bf16[4,8,64,128]{3,2,1,0:T(8,128)(2,1)S(1)} %get-tuple-element.79), channel_id=1, source_target_pairs={{0,130},{2,128},{128,2},{130,0},{1,131},{3,129},{129,3},{131,1},{4... | collective-permute-start | bytes 1572872 | tf_op jit(solution)/shard_map/reduce1/ppermute | solution.py:329
  44.9 1.1 %collective-permute-start.13 = (bf16[4,8,64,128]{3,2,1,0:T(8,128)(2,1)S(1)}, bf16[4,8,64,128]{3,2,1,0:T(8,128)(2,1)S(1)}, u32[]{:S(2)}, u32[]{:S(2)}) collective-permute-start(bf16[4,8,64,128]{3,2,1,0:T(8,128)(2,1)S(1)} %get-tuple-element.80), channel_id=1, source_target_pairs={{32,0},{64,32},{96,64},{0,96},{33,1},{65,33},{97,65},{1,97},{34,2}... | collective-permute-start | bytes 1572872 | tf_op jit(solution)/shard_map/reduce1/ppermute | solution.py:333
  46.0 1.4 %collective-permute-start.14 = (bf16[4,8,64,128]{3,2,1,0:T(8,128)(2,1)S(1)}, bf16[4,8,64,128]{3,2,1,0:T(8,128)(2,1)S(1)}, u32[]{:S(2)}, u32[]{:S(2)}) collective-permute-start(bf16[4,8,64,128]{3,2,1,0:T(8,128)(2,1)S(1)} %get-tuple-element.81), channel_id=1, source_target_pairs={{0,128},{2,130},{128,0},{130,2},{1,129},{3,131},{129,1},{131,3},{4... | collective-permute-start | bytes 1572872 | tf_op jit(solution)/shard_map/reduce1/ppermute | solution.py:329
  47.4 10.2 %collective-permute-done.10.refs_2_ = bf16[4,8,64,128]{3,2,1,0:T(8,128)(2,1)S(1)} collective-permute-done((bf16[4,8,64,128]{3,2,1,0:T(8,128)(2,1)S(1)}, bf16[4,8,64,128]{3,2,1,0:T(8,128)(2,1)S(1)}, u32[]{:S(2)}, u32[]{:S(2)}) %collective-permute-start.10) | collective-permute-done | bytes 524320 | tf_op jit(solution)/shard_map/reduce1/ppermute | solution.py:329
  57.7 0.5 collective-permute-start.15
  58.2 0.7 collective-permute-done.11.refs_3_
  58.9 9.2 %collective-permute-done.12.refs_4_ = bf16[4,8,64,128]{3,2,1,0:T(8,128)(2,1)S(1)} collective-permute-done((bf16[4,8,64,128]{3,2,1,0:T(8,128)(2,1)S(1)}, bf16[4,8,64,128]{3,2,1,0:T(8,128)(2,1)S(1)}, u32[]{:S(2)}, u32[]{:S(2)}) %collective-permute-start.12) | collective-permute-done | bytes 524320 | tf_op jit(solution)/shard_map/reduce1/ppermute | solution.py:329
  68.1 0.9 collective-permute-done.13.refs_5_
  69.0 1.1 %collective-permute-done.15.refs_7_ = bf16[4,8,64,128]{3,2,1,0:T(8,128)(2,1)S(1)} collective-permute-done((bf16[4,8,64,128]{3,2,1,0:T(8,128)(2,1)S(1)}, bf16[4,8,64,128]{3,2,1,0:T(8,128)(2,1)S(1)}, u32[]{:S(2)}, u32[]{:S(2)}) %collective-permute-start.15) | collective-permute-done | bytes 524320 | tf_op jit(solution)/shard_map/reduce1/ppermute | solution.py:333
  70.5 1.3 %collective-permute-start.16 = (bf16[8,64,128]{2,1,0:T(8,128)(2,1)S(1)}, bf16[8,64,128]{2,1,0:T(8,128)(2,1)S(1)}, u32[]{:S(2)}, u32[]{:S(2)}) collective-permute-start(bf16[8,64,128]{2,1,0:T(8,128)(2,1)S(1)} %get-tuple-element.85), channel_id=1, source_target_pairs={{64,0},{96,32},{0,64},{32,96},{65,1},{97,33},{1,65},{33,97},{66,2}... | collective-permute-start | bytes 393224 | tf_op jit(solution)/shard_map/reduce2/ppermute | solution.py:333
  71.9 1.3 %collective-permute-start.17 = (bf16[8,64,128]{2,1,0:T(8,128)(2,1)S(1)}, bf16[8,64,128]{2,1,0:T(8,128)(2,1)S(1)}, u32[]{:S(2)}, u32[]{:S(2)}) collective-permute-start(bf16[8,64,128]{2,1,0:T(8,128)(2,1)S(1)} %get-tuple-element.86), channel_id=1, source_target_pairs={{0,2},{2,0},{128,130},{130,128},{1,3},{3,1},{129,131},{131,129},{4... | collective-permute-start | bytes 393224 | tf_op jit(solution)/shard_map/reduce2/ppermute | solution.py:329
  73.2 1.4 %collective-permute-start.18 = (bf16[8,64,128]{2,1,0:T(8,128)(2,1)S(1)}, bf16[8,64,128]{2,1,0:T(8,128)(2,1)S(1)}, u32[]{:S(2)}, u32[]{:S(2)}) collective-permute-start(bf16[8,64,128]{2,1,0:T(8,128)(2,1)S(1)} %get-tuple-element.87), channel_id=1, source_target_pairs={{32,0},{64,32},{96,64},{0,96},{33,1},{65,33},{97,65},{1,97},{34,2}... | collective-permute-start | bytes 393224 | tf_op jit(solution)/shard_map/reduce2/ppermute | solution.py:333
  74.6 2.1 %collective-permute-start.19 = (bf16[8,64,128]{2,1,0:T(8,128)(2,1)S(1)}, bf16[8,64,128]{2,1,0:T(8,128)(2,1)S(1)}, u32[]{:S(2)}, u32[]{:S(2)}) collective-permute-start(bf16[8,64,128]{2,1,0:T(8,128)(2,1)S(1)} %get-tuple-element.88), channel_id=1, source_target_pairs={{0,130},{2,128},{128,2},{130,0},{1,131},{3,129},{129,3},{131,1},{4... | collective-permute-start | bytes 393224 | tf_op jit(solution)/shard_map/reduce2/ppermute | solution.py:329
  76.7 0.6 collective-permute-start.20
  77.3 1.1 %collective-permute-done.16.refs_2_ = bf16[8,64,128]{2,1,0:T(8,128)(2,1)S(1)} collective-permute-done((bf16[8,64,128]{2,1,0:T(8,128)(2,1)S(1)}, bf16[8,64,128]{2,1,0:T(8,128)(2,1)S(1)}, u32[]{:S(2)}, u32[]{:S(2)}) %collective-permute-start.16) | collective-permute-done | bytes 131104 | tf_op jit(solution)/shard_map/reduce2/ppermute | solution.py:333
  78.4 0.5 collective-permute-start.21
  79.4 1.4 %collective-permute-done.19.refs_5_ = bf16[8,64,128]{2,1,0:T(8,128)(2,1)S(1)} collective-permute-done((bf16[8,64,128]{2,1,0:T(8,128)(2,1)S(1)}, bf16[8,64,128]{2,1,0:T(8,128)(2,1)S(1)}, u32[]{:S(2)}, u32[]{:S(2)}) %collective-permute-start.19) | collective-permute-done | bytes 131104 | tf_op jit(solution)/shard_map/reduce2/ppermute | solution.py:329
  80.8 0.9 collective-permute-done.20.refs_6_
  81.7 1.7 %collective-permute-done.21.refs_7_ = bf16[8,64,128]{2,1,0:T(8,128)(2,1)S(1)} collective-permute-done((bf16[8,64,128]{2,1,0:T(8,128)(2,1)S(1)}, bf16[8,64,128]{2,1,0:T(8,128)(2,1)S(1)}, u32[]{:S(2)}, u32[]{:S(2)}) %collective-permute-start.21) | collective-permute-done | bytes 131104 | tf_op jit(solution)/shard_map/reduce2/ppermute | solution.py:329
  83.5 7.1 %collective-permute-start.22 = (f32[128,128]{1,0:T(8,128)S(1)}, f32[128,128]{1,0:T(8,128)S(1)}, u32[]{:S(2)}, u32[]{:S(2)}) collective-permute-start(f32[128,128]{1,0:T(8,128)S(1)} %get-tuple-element.92), channel_id=1, source_target_pairs={{16,0},{20,4},{24,8},{28,12},{0,16},{4,20},{8,24},{12,28},{17,1},{... | collective-permute-start | bytes 196616 | tf_op jit(solution)/shard_map/reduce3/ppermute | solution.py:337
  90.6 1.9 %collective-permute-start.23 = (f32[128,128]{1,0:T(8,128)S(1)}, f32[128,128]{1,0:T(8,128)S(1)}, u32[]{:S(2)}, u32[]{:S(2)}) collective-permute-start(f32[128,128]{1,0:T(8,128)S(1)} %get-tuple-element.93), channel_id=1, source_target_pairs={{20,0},{24,4},{28,8},{0,12},{4,16},{8,20},{12,24},{16,28},{21,1},{... | collective-permute-start | bytes 196616 | tf_op jit(solution)/shard_map/reduce3/ppermute | solution.py:337
  92.5 3.1 %collective-permute-start.24 = (f32[128,128]{1,0:T(8,128)S(1)}, f32[128,128]{1,0:T(8,128)S(1)}, u32[]{:S(2)}, u32[]{:S(2)}) collective-permute-start(f32[128,128]{1,0:T(8,128)S(1)} %get-tuple-element.94), channel_id=1, source_target_pairs={{12,0},{16,4},{20,8},{24,12},{28,16},{0,20},{4,24},{8,28},{13,1},{... | collective-permute-start | bytes 196616 | tf_op jit(solution)/shard_map/reduce3/ppermute | solution.py:337
  95.6 1.5 %collective-permute-start.25 = (f32[128,128]{1,0:T(8,128)S(1)}, f32[128,128]{1,0:T(8,128)S(1)}, u32[]{:S(2)}, u32[]{:S(2)}) collective-permute-start(f32[128,128]{1,0:T(8,128)S(1)} %get-tuple-element.95), channel_id=1, source_target_pairs={{24,0},{28,4},{0,8},{4,12},{8,16},{12,20},{16,24},{20,28},{25,1},{... | collective-permute-start | bytes 196616 | tf_op jit(solution)/shard_map/reduce3/ppermute | solution.py:337
  97.1 2.6 %collective-permute-start.26 = (f32[128,128]{1,0:T(8,128)S(1)}, f32[128,128]{1,0:T(8,128)S(1)}, u32[]{:S(2)}, u32[]{:S(2)}) collective-permute-start(f32[128,128]{1,0:T(8,128)S(1)} %get-tuple-element.96), channel_id=1, source_target_pairs={{8,0},{12,4},{16,8},{20,12},{24,16},{28,20},{0,24},{4,28},{9,1},{1... | collective-permute-start | bytes 196616 | tf_op jit(solution)/shard_map/reduce3/ppermute | solution.py:337
  99.8 1.0 collective-permute-start.27
  100.8 2.2 %collective-permute-start.28 = (f32[128,128]{1,0:T(8,128)S(1)}, f32[128,128]{1,0:T(8,128)S(1)}, u32[]{:S(2)}, u32[]{:S(2)}) collective-permute-start(f32[128,128]{1,0:T(8,128)S(1)} %get-tuple-element.98), channel_id=1, source_target_pairs={{4,0},{8,4},{12,8},{16,12},{20,16},{24,20},{28,24},{0,28},{5,1},{9... | collective-permute-start | bytes 196616 | tf_op jit(solution)/shard_map/reduce3/ppermute | solution.py:337
  103.0 2.2 %collective-permute-done.27.refs_6_ = f32[128,128]{1,0:T(8,128)S(1)} collective-permute-done((f32[128,128]{1,0:T(8,128)S(1)}, f32[128,128]{1,0:T(8,128)S(1)}, u32[]{:S(2)}, u32[]{:S(2)}) %collective-permute-start.27) | collective-permute-done | bytes 65568 | tf_op jit(solution)/shard_map/reduce3/ppermute | solution.py:337
  105.3 0.8 means.1
  (37 shorter events, 2.4 us)
Async XLA Ops:
  0.0 11.4 %collective-permute-start = (bf16[448,4096]{1,0:T(8,128)(2,1)}, bf16[448,4096]{1,0:T(8,128)(2,1)}, u32[]{:S(2)}, u32[]{:S(2)}) collective-permute-start(bf16[448,4096]{1,0:T(8,128)(2,1)} %p_ref.1), channel_id=1, source_target_pairs={{0,1},{1,0},{2,3},{3,2},{4,5},{5,4},{6,7},{7,6},{8,9},{9,8},{10,11... | collective-permute-start | bytes 11010056 | tf_op jit(solution)/shard_map/swap/ppermute | solution.py:347
  1.1 10.3 %collective-permute-start.1 = (bf16[240,512]{1,0:T(8,128)(2,1)S(1)}, bf16[240,512]{1,0:T(8,128)(2,1)S(1)}, u32[]{:S(2)}, u32[]{:S(2)}) collective-permute-start(bf16[240,512]{1,0:T(8,128)(2,1)S(1)} %get-tuple-element.52), channel_id=1, source_target_pairs={{0,130},{2,128},{128,2},{130,0},{1,131},{3,129},{129,3},{131,1},{4... | collective-permute-start | bytes 737288 | tf_op jit(solution)/shard_map/references/ppermute | solution.py:352
  4.7 2.2 %collective-permute-start.2 = (f32[8,512]{1,0:T(8,128)S(1)}, f32[8,512]{1,0:T(8,128)S(1)}, u32[]{:S(2)}, u32[]{:S(2)}) collective-permute-start(f32[8,512]{1,0:T(8,128)S(1)} %pad.4.meta_ref.meta_a), channel_id=1, source_target_pairs={{0,1},{1,0},{2,3},{3,2},{4,5},{5,4},{6,7},{7,6},{8,9},{9,8},{10,11... | collective-permute-start | bytes 49160 | tf_op jit(solution)/shard_map/swap/ppermute | solution.py:356
  6.9 17.5 %collective-permute-start.3 = (bf16[240,512]{1,0:T(8,128)(2,1)S(1)}, bf16[240,512]{1,0:T(8,128)(2,1)S(1)}, u32[]{:S(2)}, u32[]{:S(2)}) collective-permute-start(bf16[240,512]{1,0:T(8,128)(2,1)S(1)} %get-tuple-element.59), channel_id=1, source_target_pairs={{0,130},{2,128},{128,2},{130,0},{1,131},{3,129},{129,3},{131,1},{4... | collective-permute-start | bytes 737288 | tf_op jit(solution)/shard_map/references/ppermute | solution.py:359
  10.3 20.9 %collective-permute-start.4 = (bf16[240,1024]{1,0:T(8,128)(2,1)S(1)}, bf16[240,1024]{1,0:T(8,128)(2,1)S(1)}, u32[]{:S(2)}, u32[]{:S(2)}) collective-permute-start(bf16[240,1024]{1,0:T(8,128)(2,1)S(1)} %slice.3), channel_id=1, source_target_pairs={{0,130},{2,128},{128,2},{130,0},{1,131},{3,129},{129,3},{131,1},{4... | collective-permute-start | bytes 1474568 | tf_op jit(solution)/shard_map/references/ppermute | solution.py:362
  11.4 19.8 %collective-permute-start.5 = (bf16[240,512]{1,0:T(8,128)(2,1)S(1)}, bf16[240,512]{1,0:T(8,128)(2,1)S(1)}, u32[]{:S(2)}, u32[]{:S(2)}) collective-permute-start(bf16[240,512]{1,0:T(8,128)(2,1)S(1)} %collective-permute-done.1.q0), channel_id=1, source_target_pairs={{32,0},{64,32},{96,64},{0,96},{33,1},{65,33},{97,65},{1,97},{34,2}... | collective-permute-start | bytes 737288 | tf_op jit(solution)/shard_map/references/ppermute | solution.py:325
  13.3 17.9 %collective-permute-start.6 = (bf16[240,512]{1,0:T(8,128)(2,1)S(1)}, bf16[240,512]{1,0:T(8,128)(2,1)S(1)}, u32[]{:S(2)}, u32[]{:S(2)}) collective-permute-start(bf16[240,512]{1,0:T(8,128)(2,1)S(1)} %collective-permute-done.1.q0), channel_id=1, source_target_pairs={{64,0},{96,32},{0,64},{32,96},{65,1},{97,33},{1,65},{33,97},{66,2}... | collective-permute-start | bytes 737288 | tf_op jit(solution)/shard_map/references/ppermute | solution.py:325
  14.4 16.8 %collective-permute-start.7 = (bf16[240,512]{1,0:T(8,128)(2,1)S(1)}, bf16[240,512]{1,0:T(8,128)(2,1)S(1)}, u32[]{:S(2)}, u32[]{:S(2)}) collective-permute-start(bf16[240,512]{1,0:T(8,128)(2,1)S(1)} %collective-permute-done.1.q0), channel_id=1, source_target_pairs={{96,0},{0,32},{32,64},{64,96},{97,1},{1,33},{33,65},{65,97},{98,2}... | collective-permute-start | bytes 737288 | tf_op jit(solution)/shard_map/references/ppermute | solution.py:325
  20.3 6.3 %copy-start = (bf16[8,30,4096]{2,0,1:T(8,128)(2,1)S(1)}, bf16[8,30,4096]{2,0,1:T(8,128)(2,1)}, u32[]{:S(2)}) copy-start(bf16[8,30,4096]{2,0,1:T(8,128)(2,1)} %param.9) | copy-start | bytes 5898244
  24.5 7.2 %collective-permute-start.8 = (bf16[240,512]{1,0:T(8,128)(2,1)S(1)}, bf16[240,512]{1,0:T(8,128)(2,1)S(1)}, u32[]{:S(2)}, u32[]{:S(2)}) collective-permute-start(bf16[240,512]{1,0:T(8,128)(2,1)S(1)} %collective-permute-done.3.z0), channel_id=1, source_target_pairs={{0,4},{4,0},{8,12},{12,8},{16,20},{20,16},{24,28},{28,24},{1,5},{5... | collective-permute-start | bytes 737288 | tf_op jit(solution)/shard_map/references/ppermute | solution.py:370
  34.6 1.3 %collective-permute-start.9 = (f32[8,1024]{1,0:T(8,128)S(1)}, f32[8,1024]{1,0:T(8,128)S(1)}, u32[]{:S(2)}, u32[]{:S(2)}) collective-permute-start(f32[8,1024]{1,0:T(8,128)S(1)} %get-tuple-element.74.mine_ref), channel_id=1, source_target_pairs={{0,1},{1,0},{2,3},{3,2},{4,5},{5,4},{6,7},{7,6},{8,9},{9,8},{10,11... | collective-permute-start | bytes 98312 | tf_op jit(solution)/shard_map/scores/ppermute | solution.py:403
  41.2 64.0 %copy-start.1 = (f32[2048]{0:T(1024)S(1)}, f32[2048]{0:T(1024)}, u32[]{:S(2)}) copy-start(f32[2048]{0:T(1024)} %param.11) | copy-start | bytes 24580
  41.2 16.4 %collective-permute-start.10 = (bf16[4,8,64,128]{3,2,1,0:T(8,128)(2,1)S(1)}, bf16[4,8,64,128]{3,2,1,0:T(8,128)(2,1)S(1)}, u32[]{:S(2)}, u32[]{:S(2)}) collective-permute-start(bf16[4,8,64,128]{3,2,1,0:T(8,128)(2,1)S(1)} %get-tuple-element.77), channel_id=1, source_target_pairs={{0,2},{2,0},{128,130},{130,128},{1,3},{3,1},{129,131},{131,129},{4... | collective-permute-start | bytes 1572872 | tf_op jit(solution)/shard_map/reduce1/ppermute | solution.py:329
  42.5 16.4 %collective-permute-start.11 = (bf16[4,8,64,128]{3,2,1,0:T(8,128)(2,1)S(1)}, bf16[4,8,64,128]{3,2,1,0:T(8,128)(2,1)S(1)}, u32[]{:S(2)}, u32[]{:S(2)}) collective-permute-start(bf16[4,8,64,128]{3,2,1,0:T(8,128)(2,1)S(1)} %get-tuple-element.78), channel_id=1, source_target_pairs={{64,0},{96,32},{0,64},{32,96},{65,1},{97,33},{1,65},{33,97},{66,2}... | collective-permute-start | bytes 1572872 | tf_op jit(solution)/shard_map/reduce1/ppermute | solution.py:333
  43.8 24.3 %collective-permute-start.12 = (bf16[4,8,64,128]{3,2,1,0:T(8,128)(2,1)S(1)}, bf16[4,8,64,128]{3,2,1,0:T(8,128)(2,1)S(1)}, u32[]{:S(2)}, u32[]{:S(2)}) collective-permute-start(bf16[4,8,64,128]{3,2,1,0:T(8,128)(2,1)S(1)} %get-tuple-element.79), channel_id=1, source_target_pairs={{0,130},{2,128},{128,2},{130,0},{1,131},{3,129},{129,3},{131,1},{4... | collective-permute-start | bytes 1572872 | tf_op jit(solution)/shard_map/reduce1/ppermute | solution.py:329
  44.9 24.1 %collective-permute-start.13 = (bf16[4,8,64,128]{3,2,1,0:T(8,128)(2,1)S(1)}, bf16[4,8,64,128]{3,2,1,0:T(8,128)(2,1)S(1)}, u32[]{:S(2)}, u32[]{:S(2)}) collective-permute-start(bf16[4,8,64,128]{3,2,1,0:T(8,128)(2,1)S(1)} %get-tuple-element.80), channel_id=1, source_target_pairs={{32,0},{64,32},{96,64},{0,96},{33,1},{65,33},{97,65},{1,97},{34,2}... | collective-permute-start | bytes 1572872 | tf_op jit(solution)/shard_map/reduce1/ppermute | solution.py:333
  46.0 23.0 %collective-permute-start.14 = (bf16[4,8,64,128]{3,2,1,0:T(8,128)(2,1)S(1)}, bf16[4,8,64,128]{3,2,1,0:T(8,128)(2,1)S(1)}, u32[]{:S(2)}, u32[]{:S(2)}) collective-permute-start(bf16[4,8,64,128]{3,2,1,0:T(8,128)(2,1)S(1)} %get-tuple-element.81), channel_id=1, source_target_pairs={{0,128},{2,130},{128,0},{130,2},{1,129},{3,131},{129,1},{131,3},{4... | collective-permute-start | bytes 1572872 | tf_op jit(solution)/shard_map/reduce1/ppermute | solution.py:329
  57.7 12.4 %collective-permute-start.15 = (bf16[4,8,64,128]{3,2,1,0:T(8,128)(2,1)S(1)}, bf16[4,8,64,128]{3,2,1,0:T(8,128)(2,1)S(1)}, u32[]{:S(2)}, u32[]{:S(2)}) collective-permute-start(bf16[4,8,64,128]{3,2,1,0:T(8,128)(2,1)S(1)} %get-tuple-element.82), channel_id=1, source_target_pairs={{96,0},{0,32},{32,64},{64,96},{97,1},{1,33},{33,65},{65,97},{98,2}... | collective-permute-start | bytes 1572872 | tf_op jit(solution)/shard_map/reduce1/ppermute | solution.py:333
  70.5 7.9 %collective-permute-start.16 = (bf16[8,64,128]{2,1,0:T(8,128)(2,1)S(1)}, bf16[8,64,128]{2,1,0:T(8,128)(2,1)S(1)}, u32[]{:S(2)}, u32[]{:S(2)}) collective-permute-start(bf16[8,64,128]{2,1,0:T(8,128)(2,1)S(1)} %get-tuple-element.85), channel_id=1, source_target_pairs={{64,0},{96,32},{0,64},{32,96},{65,1},{97,33},{1,65},{33,97},{66,2}... | collective-permute-start | bytes 393224 | tf_op jit(solution)/shard_map/reduce2/ppermute | solution.py:333
  71.9 7.1 %collective-permute-start.17 = (bf16[8,64,128]{2,1,0:T(8,128)(2,1)S(1)}, bf16[8,64,128]{2,1,0:T(8,128)(2,1)S(1)}, u32[]{:S(2)}, u32[]{:S(2)}) collective-permute-start(bf16[8,64,128]{2,1,0:T(8,128)(2,1)S(1)} %get-tuple-element.86), channel_id=1, source_target_pairs={{0,2},{2,0},{128,130},{130,128},{1,3},{3,1},{129,131},{131,129},{4... | collective-permute-start | bytes 393224 | tf_op jit(solution)/shard_map/reduce2/ppermute | solution.py:329
  73.2 6.3 %collective-permute-start.18 = (bf16[8,64,128]{2,1,0:T(8,128)(2,1)S(1)}, bf16[8,64,128]{2,1,0:T(8,128)(2,1)S(1)}, u32[]{:S(2)}, u32[]{:S(2)}) collective-permute-start(bf16[8,64,128]{2,1,0:T(8,128)(2,1)S(1)} %get-tuple-element.87), channel_id=1, source_target_pairs={{32,0},{64,32},{96,64},{0,96},{33,1},{65,33},{97,65},{1,97},{34,2}... | collective-permute-start | bytes 393224 | tf_op jit(solution)/shard_map/reduce2/ppermute | solution.py:333
  74.6 6.2 %collective-permute-start.19 = (bf16[8,64,128]{2,1,0:T(8,128)(2,1)S(1)}, bf16[8,64,128]{2,1,0:T(8,128)(2,1)S(1)}, u32[]{:S(2)}, u32[]{:S(2)}) collective-permute-start(bf16[8,64,128]{2,1,0:T(8,128)(2,1)S(1)} %get-tuple-element.88), channel_id=1, source_target_pairs={{0,130},{2,128},{128,2},{130,0},{1,131},{3,129},{129,3},{131,1},{4... | collective-permute-start | bytes 393224 | tf_op jit(solution)/shard_map/reduce2/ppermute | solution.py:329
  76.7 5.0 %collective-permute-start.20 = (bf16[8,64,128]{2,1,0:T(8,128)(2,1)S(1)}, bf16[8,64,128]{2,1,0:T(8,128)(2,1)S(1)}, u32[]{:S(2)}, u32[]{:S(2)}) collective-permute-start(bf16[8,64,128]{2,1,0:T(8,128)(2,1)S(1)} %get-tuple-element.89), channel_id=1, source_target_pairs={{96,0},{0,32},{32,64},{64,96},{97,1},{1,33},{33,65},{65,97},{98,2}... | collective-permute-start | bytes 393224 | tf_op jit(solution)/shard_map/reduce2/ppermute | solution.py:333
  78.4 5.0 %collective-permute-start.21 = (bf16[8,64,128]{2,1,0:T(8,128)(2,1)S(1)}, bf16[8,64,128]{2,1,0:T(8,128)(2,1)S(1)}, u32[]{:S(2)}, u32[]{:S(2)}) collective-permute-start(bf16[8,64,128]{2,1,0:T(8,128)(2,1)S(1)} %get-tuple-element.90), channel_id=1, source_target_pairs={{0,128},{2,130},{128,0},{130,2},{1,129},{3,131},{129,1},{131,3},{4... | collective-permute-start | bytes 393224 | tf_op jit(solution)/shard_map/reduce2/ppermute | solution.py:329
  83.5 16.3 %collective-permute-start.22 = (f32[128,128]{1,0:T(8,128)S(1)}, f32[128,128]{1,0:T(8,128)S(1)}, u32[]{:S(2)}, u32[]{:S(2)}) collective-permute-start(f32[128,128]{1,0:T(8,128)S(1)} %get-tuple-element.92), channel_id=1, source_target_pairs={{16,0},{20,4},{24,8},{28,12},{0,16},{4,20},{8,24},{12,28},{17,1},{... | collective-permute-start | bytes 196616 | tf_op jit(solution)/shard_map/reduce3/ppermute | solution.py:337
  90.6 10.2 %collective-permute-start.23 = (f32[128,128]{1,0:T(8,128)S(1)}, f32[128,128]{1,0:T(8,128)S(1)}, u32[]{:S(2)}, u32[]{:S(2)}) collective-permute-start(f32[128,128]{1,0:T(8,128)S(1)} %get-tuple-element.93), channel_id=1, source_target_pairs={{20,0},{24,4},{28,8},{0,12},{4,16},{8,20},{12,24},{16,28},{21,1},{... | collective-permute-start | bytes 196616 | tf_op jit(solution)/shard_map/reduce3/ppermute | solution.py:337
  92.5 10.5 %collective-permute-start.24 = (f32[128,128]{1,0:T(8,128)S(1)}, f32[128,128]{1,0:T(8,128)S(1)}, u32[]{:S(2)}, u32[]{:S(2)}) collective-permute-start(f32[128,128]{1,0:T(8,128)S(1)} %get-tuple-element.94), channel_id=1, source_target_pairs={{12,0},{16,4},{20,8},{24,12},{28,16},{0,20},{4,24},{8,28},{13,1},{... | collective-permute-start | bytes 196616 | tf_op jit(solution)/shard_map/reduce3/ppermute | solution.py:337
  95.6 7.4 %collective-permute-start.25 = (f32[128,128]{1,0:T(8,128)S(1)}, f32[128,128]{1,0:T(8,128)S(1)}, u32[]{:S(2)}, u32[]{:S(2)}) collective-permute-start(f32[128,128]{1,0:T(8,128)S(1)} %get-tuple-element.95), channel_id=1, source_target_pairs={{24,0},{28,4},{0,8},{4,12},{8,16},{12,20},{16,24},{20,28},{25,1},{... | collective-permute-start | bytes 196616 | tf_op jit(solution)/shard_map/reduce3/ppermute | solution.py:337
  97.1 5.9 %collective-permute-start.26 = (f32[128,128]{1,0:T(8,128)S(1)}, f32[128,128]{1,0:T(8,128)S(1)}, u32[]{:S(2)}, u32[]{:S(2)}) collective-permute-start(f32[128,128]{1,0:T(8,128)S(1)} %get-tuple-element.96), channel_id=1, source_target_pairs={{8,0},{12,4},{16,8},{20,12},{24,16},{28,20},{0,24},{4,28},{9,1},{1... | collective-permute-start | bytes 196616 | tf_op jit(solution)/shard_map/reduce3/ppermute | solution.py:337
  99.8 5.5 %collective-permute-start.27 = (f32[128,128]{1,0:T(8,128)S(1)}, f32[128,128]{1,0:T(8,128)S(1)}, u32[]{:S(2)}, u32[]{:S(2)}) collective-permute-start(f32[128,128]{1,0:T(8,128)S(1)} %get-tuple-element.97), channel_id=1, source_target_pairs={{28,0},{0,4},{4,8},{8,12},{12,16},{16,20},{20,24},{24,28},{29,1},{... | collective-permute-start | bytes 196616 | tf_op jit(solution)/shard_map/reduce3/ppermute | solution.py:337
  100.8 4.4 %collective-permute-start.28 = (f32[128,128]{1,0:T(8,128)S(1)}, f32[128,128]{1,0:T(8,128)S(1)}, u32[]{:S(2)}, u32[]{:S(2)}) collective-permute-start(f32[128,128]{1,0:T(8,128)S(1)} %get-tuple-element.98), channel_id=1, source_target_pairs={{4,0},{8,4},{12,8},{16,12},{20,16},{24,20},{28,24},{0,28},{5,1},{9... | collective-permute-start | bytes 196616 | tf_op jit(solution)/shard_map/reduce3/ppermute | solution.py:337

commit v3 on v2

--- a/solution.py
+++ b/solution.py
@@ -366,7 +366,7 @@
         oth = shift_particles(raw, meta_oth, 12)
     with jax.named_scope("references"):
         quarters = [from_y(crossed, s) for s in (1, 2, 3)]
-        z_crossed, oth = lax.optimization_barrier((z_crossed, oth))
+        z_crossed, own = lax.optimization_barrier((z_crossed, own))
         z_other = lax.ppermute(z_crossed, "z", [(i, i ^ 1) for i in range(8)])
     inv = (1.0 / jnp.concatenate([sigma2, sigma2])).reshape(1, WIDE)
     log_prior = jnp.log(class_prior).reshape(2, 2, 8)
@@ -445,7 +445,7 @@
             compiler_params=pltpu.CompilerParams(vmem_limit_bytes=4 * MB),
         )(*[piece for pair in zip(*pieces) for piece in pair])
     with jax.named_scope("reduce3"):
-        owned = [slots[0]] + [to_z(slots[s], s) for s in (4, 3, 5, 2, 6, 1, 7)]
+        owned = [slots[0]] + [to_z(slots[s], s) for s in (1, 7, 2, 6, 3, 5, 4)]
 
     with jax.named_scope("means"):
         d = (x_lo * 4 + y) * 8 + z

time: 106 us -> 109 us (1.028); the launches traced: 106 us -> 108 us
  waiting for transfers between devices: 31.4 us -> 32.9 us
    ppermute x6, waiting for transfers between devices: 22.5 us -> 20.9 us  [to_x(): lax.ppermute(value, X, [(i, i ^ flips >> 1 ^ (flips & 1) << 1) for i in r...]
    ppermute x7, waiting for transfers between devices: 2.24 us -> 3.72 us  [to_z(): return lax.ppermute(value, 'z', ring(8, -step))]
    ppermute x6, starting transfers between devices: 7.8 us -> 9.28 us  [to_x(): lax.ppermute(value, X, [(i, i ^ flips >> 1 ^ (flips & 1) << 1) for i in r...]
    ppermute x6, waiting for transfers between devices: 5.11 us -> 6.42 us  [to_y(): return lax.ppermute(value, 'y', ring(4, -step))]
    ppermute x6, starting transfers between devices: 6.25 us -> 5.12 us  [to_y(): return lax.ppermute(value, 'y', ring(4, -step))]
where the time goes in v3:
time: 109 us; the launch traced here: 108 us
  starting transfers between devices  47.6 us (44%)
  waiting for transfers between devices  32.9 us (30%)
  Pallas kernels  22.2 us (20%)
  local copies, waits for them, and re-layouts  3.12 us (3%)
  other arithmetic  1.75 us (2%)
    ppermute x6, waiting for transfers between devices, to_x(): lax.ppermute(value, X, [(i, i ^ flips >> 1 ^ (flips & 1) << 1) for i in r...  20.9 us
    ppermute x7, starting transfers between devices, to_z(): return lax.ppermute(value, 'z', ring(8, -step))  19.1 us
    ppermute x6, starting transfers between devices, to_x(): lax.ppermute(value, X, [(i, i ^ flips >> 1 ^ (flips & 1) << 1) for i in r...  9.28 us
    pallas_call x2, Pallas kernels, shift_particles(): pl.pallas_call(shift_kernel, out_shape=jax.ShapeDtypeStruct((NP, WIDE), B...  7.94 us
    ppermute x6, waiting for transfers between devices, to_y(): return lax.ppermute(value, 'y', ring(4, -step))  6.42 us
    pallas_call x1, Pallas kernels, local(): pl.pallas_call(sums_kernel, out_shape=([jax.ShapeDtypeStruct((4, 8, PROWS...  5.31 us
    ppermute x6, starting transfers between devices, to_y(): return lax.ppermute(value, 'y', ring(4, -step))  5.12 us
    ppermute x3, starting transfers between devices, from_y(): return lax.ppermute(value, 'y', ring(4, step))  4.93 us
  transfers between devices with their start and end apart: 29, of which 13 were waited for; matrix products, arithmetic and copies ran while one was open for 5% of the time, Pallas kernels for 12%

profile of v3, /device:TPU:8, one launch (start us, length us, event | category | flops | bytes accessed | tf_op | source)
XLA Modules:
  0.0 107.8 jit_solution(2791567262328033316)
XLA Ops:
  0.0 1.1 %constant_dynamic-slice_fusion.2 = (bf16[240,512]{1,0:T(8,128)(2,1)S(1)}, bf16[240,512]{1,0:T(8,128)(2,1)S(1)}) fusion(bf16[240,4096]{1,0:T(8,128)(2,1)} %bitcast.21, s32[]{:T(128)S(6)} %select_n.17, s32[]{:T(128)S(6)} %select_n.16), kind=kLoop, calls=%fused_computation.4 | loop fusion | bytes 983048 | tf_op jit(solution)/shard_map/references/dynamic_slice | solution.py:350
  1.1 0.7 add_convert_fusion
  1.8 0.6 collective-permute-start
  2.4 2.8 %collective-permute-start.3 = (bf16[240,512]{1,0:T(8,128)(2,1)S(1)}, bf16[240,512]{1,0:T(8,128)(2,1)S(1)}, u32[]{:S(2)}, u32[]{:S(2)}) collective-permute-start(bf16[240,512]{1,0:T(8,128)(2,1)S(1)} %get-tuple-element.56), channel_id=1, source_target_pairs={{0,130},{2,128},{128,2},{130,0},{1,131},{3,129},{129,3},{131,1},{4... | collective-permute-start | bytes 737288 | tf_op jit(solution)/shard_map/references/ppermute | solution.py:352
  5.2 0.8 maximum_divide_fusion.inv_ref
  6.1 0.7 log.3
  7.1 2.1 %collective-permute-start.1 = (bf16[240,512]{1,0:T(8,128)(2,1)S(1)}, bf16[240,512]{1,0:T(8,128)(2,1)S(1)}, u32[]{:S(2)}, u32[]{:S(2)}) collective-permute-start(bf16[240,512]{1,0:T(8,128)(2,1)S(1)} %get-tuple-element.55), channel_id=1, source_target_pairs={{0,130},{2,128},{128,2},{130,0},{1,131},{3,129},{129,3},{131,1},{4... | collective-permute-start | bytes 737288 | tf_op jit(solution)/shard_map/references/ppermute | solution.py:359
  9.2 1.1 slice.3
  10.3 1.3 %collective-permute-start.4 = (bf16[240,1024]{1,0:T(8,128)(2,1)S(1)}, bf16[240,1024]{1,0:T(8,128)(2,1)S(1)}, u32[]{:S(2)}, u32[]{:S(2)}) collective-permute-start(bf16[240,1024]{1,0:T(8,128)(2,1)S(1)} %slice.3), channel_id=1, source_target_pairs={{0,130},{2,128},{128,2},{130,0},{1,131},{3,129},{129,3},{131,1},{4... | collective-permute-start | bytes 1474568 | tf_op jit(solution)/shard_map/references/ppermute | solution.py:362
  11.6 0.7 collective-permute-done.3.q0
  12.3 2.3 %collective-permute-start.5 = (bf16[240,512]{1,0:T(8,128)(2,1)S(1)}, bf16[240,512]{1,0:T(8,128)(2,1)S(1)}, u32[]{:S(2)}, u32[]{:S(2)}) collective-permute-start(bf16[240,512]{1,0:T(8,128)(2,1)S(1)} %collective-permute-done.3.q0), channel_id=1, source_target_pairs={{32,0},{64,32},{96,64},{0,96},{33,1},{65,33},{97,65},{1,97},{34,2}... | collective-permute-start | bytes 737288 | tf_op jit(solution)/shard_map/references/ppermute | solution.py:325
  14.6 0.7 collective-permute-start.6
  15.3 1.9 %collective-permute-start.7 = (bf16[240,512]{1,0:T(8,128)(2,1)S(1)}, bf16[240,512]{1,0:T(8,128)(2,1)S(1)}, u32[]{:S(2)}, u32[]{:S(2)}) collective-permute-start(bf16[240,512]{1,0:T(8,128)(2,1)S(1)} %collective-permute-done.3.q0), channel_id=1, source_target_pairs={{96,0},{0,32},{32,64},{64,96},{97,1},{1,33},{33,65},{65,97},{98,2}... | collective-permute-start | bytes 737288 | tf_op jit(solution)/shard_map/references/ppermute | solution.py:325
  17.2 4.0 %shift.2.own_ref = bf16[448,4096]{1,0:T(8,128)(2,1)S(1)} custom-call(f32[8,512]{1,0:T(8,128)S(1)} %pad.4.meta_ref.meta_a, bf16[448,4096]{1,0:T(8,128)(2,1)} %p_ref.1), custom_call_target="tpu_custom_call" | custom-call | flops 5000000000 | tf_op jit(solution)/shard_map/shift/pallas_call | solution.py:83
  21.2 2.2 %collective-permute-start.8 = (bf16[240,512]{1,0:T(8,128)(2,1)S(1)}, bf16[240,512]{1,0:T(8,128)(2,1)S(1)}, u32[]{:S(2)}, u32[]{:S(2)}) collective-permute-start(bf16[240,512]{1,0:T(8,128)(2,1)S(1)} %collective-permute-done.1.z0), channel_id=1, source_target_pairs={{0,4},{4,0},{8,12},{12,8},{16,20},{20,16},{24,28},{28,24},{1,5},{5... | collective-permute-start | bytes 737288 | tf_op jit(solution)/shard_map/references/ppermute | solution.py:370
  23.4 4.0 %shift.3.oth_ref = bf16[448,4096]{1,0:T(8,128)(2,1)S(1)} custom-call(f32[8,512]{1,0:T(8,128)S(1)} %collective-permute-done.meta_ref.meta_b, bf16[448,4096]{1,0:T(8,128)(2,1)} %collective-permute-done.2.p_ref), custom_call_target="tpu_custom_call" | custom-call | flops 5000000000 | tf_op jit(solution)/shard_map/shift/pallas_call | solution.py:83
  27.4 4.6 %scores.2 = (bf16[1024,4096]{1,0:T(8,128)(2,1)S(1)}, f32[8,240,128]{2,1,0:T(8,128)S(1)}, f32[8,1024]{1,0:T(8,128)S(1)}, f32[8,240,128]{2,1,0:T(8,128)S(1)}, f32[240,128]{1,0:T(8,128)S(1)}) custom-call(s32[2]{0:T(128)S(1)} %pad_add_fusion.1.where_ref, bf16[448,4096]{1,0:T(8,128)(2,1)S(1)} %shift.2.own_ref, bf16[448,4096]{1,0:T(8,128)(2,1)S(1)} %shift.3.oth_ref, ...), custom_call_target="tpu_custom_call" | custom-call | flops 7000000000 | tf_op jit(solution)/shard_map/scores/pallas_call | solution.py:382
  32.0 3.0 %scores.3 = (f32[8,240,128]{2,1,0:T(8,128)S(1)}, f32[8,1024]{1,0:T(8,128)S(1)}) custom-call(s32[4]{0:T(128)S(1)} %pad_add_fusion.2.where_ref, bf16[1024,4096]{1,0:T(8,128)(2,1)S(1)} %get-tuple-element.68.w_ref, f32[1,4096]{1,0:T(1,128)S(1)} %maximum_divide_fusion.inv_ref, f32[240,1]{1,0:T(8,128)S(1)} %reshape_tile.9.bias_ref, ...), custom_call_target="tpu_custom_call" | custom-call | flops 5000000000 | tf_op jit(solution)/shard_map/scores/pallas_call | solution.py:391
  35.4 1.1 %collective-permute-done.9.theirs_ref = f32[8,1024]{1,0:T(8,128)S(1)} collective-permute-done((f32[8,1024]{1,0:T(8,128)S(1)}, f32[8,1024]{1,0:T(8,128)S(1)}, u32[]{:S(2)}, u32[]{:S(2)}) %collective-permute-start.9) | collective-permute-done | bytes 32800 | tf_op jit(solution)/shard_map/scores/ppermute | solution.py:403
  36.5 5.3 %sums.1 = (f32[4,8,64,128]{3,2,1,0:T(8,128)S(1)}, bf16[4,8,64,128]{3,2,1,0:T(8,128)(2,1)S(1)}, bf16[4,8,64,128]{3,2,1,0:T(8,128)(2,1)S(1)}, bf16[4,8,64,128]{3,2...) custom-call(s32[4]{0:T(128)S(1)} %pad_add_fusion.where_ref, ...), custom_call_target="tpu_custom_call" | custom-call | flops 6000000000 | tf_op jit(solution)/shard_map/sums/pallas_call | solution.py:406
  41.8 2.1 %collective-permute-start.10 = (bf16[4,8,64,128]{3,2,1,0:T(8,128)(2,1)S(1)}, bf16[4,8,64,128]{3,2,1,0:T(8,128)(2,1)S(1)}, u32[]{:S(2)}, u32[]{:S(2)}) collective-permute-start(bf16[4,8,64,128]{3,2,1,0:T(8,128)(2,1)S(1)} %get-tuple-element.77), channel_id=1, source_target_pairs={{0,2},{2,0},{128,130},{130,128},{1,3},{3,1},{129,131},{131,129},{4... | collective-permute-start | bytes 1572872 | tf_op jit(solution)/shard_map/reduce1/ppermute | solution.py:329
  43.9 1.3 %collective-permute-start.11 = (bf16[4,8,64,128]{3,2,1,0:T(8,128)(2,1)S(1)}, bf16[4,8,64,128]{3,2,1,0:T(8,128)(2,1)S(1)}, u32[]{:S(2)}, u32[]{:S(2)}) collective-permute-start(bf16[4,8,64,128]{3,2,1,0:T(8,128)(2,1)S(1)} %get-tuple-element.78), channel_id=1, source_target_pairs={{64,0},{96,32},{0,64},{32,96},{65,1},{97,33},{1,65},{33,97},{66,2}... | collective-permute-start | bytes 1572872 | tf_op jit(solution)/shard_map/reduce1/ppermute | solution.py:333
  45.1 1.1 %collective-permute-start.12 = (bf16[4,8,64,128]{3,2,1,0:T(8,128)(2,1)S(1)}, bf16[4,8,64,128]{3,2,1,0:T(8,128)(2,1)S(1)}, u32[]{:S(2)}, u32[]{:S(2)}) collective-permute-start(bf16[4,8,64,128]{3,2,1,0:T(8,128)(2,1)S(1)} %get-tuple-element.79), channel_id=1, source_target_pairs={{0,130},{2,128},{128,2},{130,0},{1,131},{3,129},{129,3},{131,1},{4... | collective-permute-start | bytes 1572872 | tf_op jit(solution)/shard_map/reduce1/ppermute | solution.py:329
  46.3 0.8 collective-permute-start.13
  47.1 0.7 collective-permute-start.14
  47.8 10.5 %collective-permute-done.10.refs_2_ = bf16[4,8,64,128]{3,2,1,0:T(8,128)(2,1)S(1)} collective-permute-done((bf16[4,8,64,128]{3,2,1,0:T(8,128)(2,1)S(1)}, bf16[4,8,64,128]{3,2,1,0:T(8,128)(2,1)S(1)}, u32[]{:S(2)}, u32[]{:S(2)}) %collective-permute-start.10) | collective-permute-done | bytes 524320 | tf_op jit(solution)/shard_map/reduce1/ppermute | solution.py:329
  58.3 2.0 %collective-permute-done.11.refs_3_ = bf16[4,8,64,128]{3,2,1,0:T(8,128)(2,1)S(1)} collective-permute-done((bf16[4,8,64,128]{3,2,1,0:T(8,128)(2,1)S(1)}, bf16[4,8,64,128]{3,2,1,0:T(8,128)(2,1)S(1)}, u32[]{:S(2)}, u32[]{:S(2)}) %collective-permute-start.11) | collective-permute-done | bytes 524320 | tf_op jit(solution)/shard_map/reduce1/ppermute | solution.py:333
  60.2 8.4 %collective-permute-done.12.refs_4_ = bf16[4,8,64,128]{3,2,1,0:T(8,128)(2,1)S(1)} collective-permute-done((bf16[4,8,64,128]{3,2,1,0:T(8,128)(2,1)S(1)}, bf16[4,8,64,128]{3,2,1,0:T(8,128)(2,1)S(1)}, u32[]{:S(2)}, u32[]{:S(2)}) %collective-permute-start.12) | collective-permute-done | bytes 524320 | tf_op jit(solution)/shard_map/reduce1/ppermute | solution.py:329
  68.6 1.7 %collective-permute-done.13.refs_5_ = bf16[4,8,64,128]{3,2,1,0:T(8,128)(2,1)S(1)} collective-permute-done((bf16[4,8,64,128]{3,2,1,0:T(8,128)(2,1)S(1)}, bf16[4,8,64,128]{3,2,1,0:T(8,128)(2,1)S(1)}, u32[]{:S(2)}, u32[]{:S(2)}) %collective-permute-start.13) | collective-permute-done | bytes 524320 | tf_op jit(solution)/shard_map/reduce1/ppermute | solution.py:333
  70.6 0.5 reduce1.1
  71.1 1.3 %collective-permute-start.16 = (bf16[8,64,128]{2,1,0:T(8,128)(2,1)S(1)}, bf16[8,64,128]{2,1,0:T(8,128)(2,1)S(1)}, u32[]{:S(2)}, u32[]{:S(2)}) collective-permute-start(bf16[8,64,128]{2,1,0:T(8,128)(2,1)S(1)} %get-tuple-element.85), channel_id=1, source_target_pairs={{64,0},{96,32},{0,64},{32,96},{65,1},{97,33},{1,65},{33,97},{66,2}... | collective-permute-start | bytes 393224 | tf_op jit(solution)/shard_map/reduce2/ppermute | solution.py:333
  72.4 2.0 %collective-permute-start.17 = (bf16[8,64,128]{2,1,0:T(8,128)(2,1)S(1)}, bf16[8,64,128]{2,1,0:T(8,128)(2,1)S(1)}, u32[]{:S(2)}, u32[]{:S(2)}) collective-permute-start(bf16[8,64,128]{2,1,0:T(8,128)(2,1)S(1)} %get-tuple-element.86), channel_id=1, source_target_pairs={{0,2},{2,0},{128,130},{130,128},{1,3},{3,1},{129,131},{131,129},{4... | collective-permute-start | bytes 393224 | tf_op jit(solution)/shard_map/reduce2/ppermute | solution.py:329
  74.4 1.1 %collective-permute-start.18 = (bf16[8,64,128]{2,1,0:T(8,128)(2,1)S(1)}, bf16[8,64,128]{2,1,0:T(8,128)(2,1)S(1)}, u32[]{:S(2)}, u32[]{:S(2)}) collective-permute-start(bf16[8,64,128]{2,1,0:T(8,128)(2,1)S(1)} %get-tuple-element.87), channel_id=1, source_target_pairs={{32,0},{64,32},{96,64},{0,96},{33,1},{65,33},{97,65},{1,97},{34,2}... | collective-permute-start | bytes 393224 | tf_op jit(solution)/shard_map/reduce2/ppermute | solution.py:333
  75.5 2.6 %collective-permute-start.19 = (bf16[8,64,128]{2,1,0:T(8,128)(2,1)S(1)}, bf16[8,64,128]{2,1,0:T(8,128)(2,1)S(1)}, u32[]{:S(2)}, u32[]{:S(2)}) collective-permute-start(bf16[8,64,128]{2,1,0:T(8,128)(2,1)S(1)} %get-tuple-element.88), channel_id=1, source_target_pairs={{0,130},{2,128},{128,2},{130,0},{1,131},{3,129},{129,3},{131,1},{4... | collective-permute-start | bytes 393224 | tf_op jit(solution)/shard_map/reduce2/ppermute | solution.py:329
  78.1 0.6 collective-permute-start.20
  79.1 0.9 collective-permute-start.21
  80.0 0.7 collective-permute-done.18.refs_4_
  80.7 1.0 collective-permute-done.19.refs_5_
  81.7 1.4 %collective-permute-done.20.refs_6_ = bf16[8,64,128]{2,1,0:T(8,128)(2,1)S(1)} collective-permute-done((bf16[8,64,128]{2,1,0:T(8,128)(2,1)S(1)}, bf16[8,64,128]{2,1,0:T(8,128)(2,1)S(1)}, u32[]{:S(2)}, u32[]{:S(2)}) %collective-permute-start.20) | collective-permute-done | bytes 131104 | tf_op jit(solution)/shard_map/reduce2/ppermute | solution.py:333
  83.1 1.0 collective-permute-done.21.refs_7_
  84.2 0.7 collective-permute-start.22
  84.8 4.8 %collective-permute-start.23 = (f32[128,128]{1,0:T(8,128)S(1)}, f32[128,128]{1,0:T(8,128)S(1)}, u32[]{:S(2)}, u32[]{:S(2)}) collective-permute-start(f32[128,128]{1,0:T(8,128)S(1)} %get-tuple-element.93), channel_id=1, source_target_pairs={{4,0},{8,4},{12,8},{16,12},{20,16},{24,20},{28,24},{0,28},{5,1},{9... | collective-permute-start | bytes 196616 | tf_op jit(solution)/shard_map/reduce3/ppermute | solution.py:337
  89.8 3.9 %collective-permute-start.25 = (f32[128,128]{1,0:T(8,128)S(1)}, f32[128,128]{1,0:T(8,128)S(1)}, u32[]{:S(2)}, u32[]{:S(2)}) collective-permute-start(f32[128,128]{1,0:T(8,128)S(1)} %get-tuple-element.95), channel_id=1, source_target_pairs={{8,0},{12,4},{16,8},{20,12},{24,16},{28,20},{0,24},{4,28},{9,1},{1... | collective-permute-start | bytes 196616 | tf_op jit(solution)/shard_map/reduce3/ppermute | solution.py:337
  93.7 0.6 collective-permute-start.26
  94.3 4.5 %collective-permute-start.27 = (f32[128,128]{1,0:T(8,128)S(1)}, f32[128,128]{1,0:T(8,128)S(1)}, u32[]{:S(2)}, u32[]{:S(2)}) collective-permute-start(f32[128,128]{1,0:T(8,128)S(1)} %get-tuple-element.97), channel_id=1, source_target_pairs={{12,0},{16,4},{20,8},{24,12},{28,16},{0,20},{4,24},{8,28},{13,1},{... | collective-permute-start | bytes 196616 | tf_op jit(solution)/shard_map/reduce3/ppermute | solution.py:337
  98.8 4.5 %collective-permute-start.28 = (f32[128,128]{1,0:T(8,128)S(1)}, f32[128,128]{1,0:T(8,128)S(1)}, u32[]{:S(2)}, u32[]{:S(2)}) collective-permute-start(f32[128,128]{1,0:T(8,128)S(1)} %get-tuple-element.98), channel_id=1, source_target_pairs={{16,0},{20,4},{24,8},{28,12},{0,16},{4,20},{8,24},{12,28},{17,1},{... | collective-permute-start | bytes 196616 | tf_op jit(solution)/shard_map/reduce3/ppermute | solution.py:337
  103.3 3.7 %collective-permute-done.28.refs_7_ = f32[128,128]{1,0:T(8,128)S(1)} collective-permute-done((f32[128,128]{1,0:T(8,128)S(1)}, f32[128,128]{1,0:T(8,128)S(1)}, u32[]{:S(2)}, u32[]{:S(2)}) %collective-permute-start.28) | collective-permute-done | bytes 65568 | tf_op jit(solution)/shard_map/reduce3/ppermute | solution.py:337
  107.0 0.8 means.1
  (37 shorter events, 1.9 us)
Async XLA Ops:
  0.0 12.3 %collective-permute-start.2 = (bf16[448,4096]{1,0:T(8,128)(2,1)}, bf16[448,4096]{1,0:T(8,128)(2,1)}, u32[]{:S(2)}, u32[]{:S(2)}) collective-permute-start(bf16[448,4096]{1,0:T(8,128)(2,1)} %p_ref.1), channel_id=1, source_target_pairs={{0,1},{1,0},{2,3},{3,2},{4,5},{5,4},{6,7},{7,6},{8,9},{9,8},{10,11... | collective-permute-start | bytes 11010056 | tf_op jit(solution)/shard_map/swap/ppermute | solution.py:347
  1.8 5.3 %collective-permute-start = (f32[8,512]{1,0:T(8,128)S(1)}, f32[8,512]{1,0:T(8,128)S(1)}, u32[]{:S(2)}, u32[]{:S(2)}) collective-permute-start(f32[8,512]{1,0:T(8,128)S(1)} %pad.4.meta_ref.meta_a), channel_id=1, source_target_pairs={{0,1},{1,0},{2,3},{3,2},{4,5},{5,4},{6,7},{7,6},{8,9},{9,8},{10,11... | collective-permute-start | bytes 49160 | tf_op jit(solution)/shard_map/swap/ppermute | solution.py:356
  2.4 9.9 %collective-permute-start.3 = (bf16[240,512]{1,0:T(8,128)(2,1)S(1)}, bf16[240,512]{1,0:T(8,128)(2,1)S(1)}, u32[]{:S(2)}, u32[]{:S(2)}) collective-permute-start(bf16[240,512]{1,0:T(8,128)(2,1)S(1)} %get-tuple-element.56), channel_id=1, source_target_pairs={{0,130},{2,128},{128,2},{130,0},{1,131},{3,129},{129,3},{131,1},{4... | collective-permute-start | bytes 737288 | tf_op jit(solution)/shard_map/references/ppermute | solution.py:352
  7.1 14.1 %collective-permute-start.1 = (bf16[240,512]{1,0:T(8,128)(2,1)S(1)}, bf16[240,512]{1,0:T(8,128)(2,1)S(1)}, u32[]{:S(2)}, u32[]{:S(2)}) collective-permute-start(bf16[240,512]{1,0:T(8,128)(2,1)S(1)} %get-tuple-element.55), channel_id=1, source_target_pairs={{0,130},{2,128},{128,2},{130,0},{1,131},{3,129},{129,3},{131,1},{4... | collective-permute-start | bytes 737288 | tf_op jit(solution)/shard_map/references/ppermute | solution.py:359
  10.3 21.7 %collective-permute-start.4 = (bf16[240,1024]{1,0:T(8,128)(2,1)S(1)}, bf16[240,1024]{1,0:T(8,128)(2,1)S(1)}, u32[]{:S(2)}, u32[]{:S(2)}) collective-permute-start(bf16[240,1024]{1,0:T(8,128)(2,1)S(1)} %slice.3), channel_id=1, source_target_pairs={{0,130},{2,128},{128,2},{130,0},{1,131},{3,129},{129,3},{131,1},{4... | collective-permute-start | bytes 1474568 | tf_op jit(solution)/shard_map/references/ppermute | solution.py:362
  12.3 19.7 %collective-permute-start.5 = (bf16[240,512]{1,0:T(8,128)(2,1)S(1)}, bf16[240,512]{1,0:T(8,128)(2,1)S(1)}, u32[]{:S(2)}, u32[]{:S(2)}) collective-permute-start(bf16[240,512]{1,0:T(8,128)(2,1)S(1)} %collective-permute-done.3.q0), channel_id=1, source_target_pairs={{32,0},{64,32},{96,64},{0,96},{33,1},{65,33},{97,65},{1,97},{34,2}... | collective-permute-start | bytes 737288 | tf_op jit(solution)/shard_map/references/ppermute | solution.py:325
  14.6 17.4 %collective-permute-start.6 = (bf16[240,512]{1,0:T(8,128)(2,1)S(1)}, bf16[240,512]{1,0:T(8,128)(2,1)S(1)}, u32[]{:S(2)}, u32[]{:S(2)}) collective-permute-start(bf16[240,512]{1,0:T(8,128)(2,1)S(1)} %collective-permute-done.3.q0), channel_id=1, source_target_pairs={{64,0},{96,32},{0,64},{32,96},{65,1},{97,33},{1,65},{33,97},{66,2}... | collective-permute-start | bytes 737288 | tf_op jit(solution)/shard_map/references/ppermute | solution.py:325
  15.3 16.7 %collective-permute-start.7 = (bf16[240,512]{1,0:T(8,128)(2,1)S(1)}, bf16[240,512]{1,0:T(8,128)(2,1)S(1)}, u32[]{:S(2)}, u32[]{:S(2)}) collective-permute-start(bf16[240,512]{1,0:T(8,128)(2,1)S(1)} %collective-permute-done.3.q0), channel_id=1, source_target_pairs={{96,0},{0,32},{32,64},{64,96},{97,1},{1,33},{33,65},{65,97},{98,2}... | collective-permute-start | bytes 737288 | tf_op jit(solution)/shard_map/references/ppermute | solution.py:325
  21.2 6.2 %copy-start = (bf16[8,30,4096]{2,0,1:T(8,128)(2,1)S(1)}, bf16[8,30,4096]{2,0,1:T(8,128)(2,1)}, u32[]{:S(2)}) copy-start(bf16[8,30,4096]{2,0,1:T(8,128)(2,1)} %param.9) | copy-start | bytes 5898244
  21.2 10.8 %collective-permute-start.8 = (bf16[240,512]{1,0:T(8,128)(2,1)S(1)}, bf16[240,512]{1,0:T(8,128)(2,1)S(1)}, u32[]{:S(2)}, u32[]{:S(2)}) collective-permute-start(bf16[240,512]{1,0:T(8,128)(2,1)S(1)} %collective-permute-done.1.z0), channel_id=1, source_target_pairs={{0,4},{4,0},{8,12},{12,8},{16,20},{20,16},{24,28},{28,24},{1,5},{5... | collective-permute-start | bytes 737288 | tf_op jit(solution)/shard_map/references/ppermute | solution.py:370
  35.0 1.5 %collective-permute-start.9 = (f32[8,1024]{1,0:T(8,128)S(1)}, f32[8,1024]{1,0:T(8,128)S(1)}, u32[]{:S(2)}, u32[]{:S(2)}) collective-permute-start(f32[8,1024]{1,0:T(8,128)S(1)} %get-tuple-element.74.mine_ref), channel_id=1, source_target_pairs={{0,1},{1,0},{2,3},{3,2},{4,5},{5,4},{6,7},{7,6},{8,9},{9,8},{10,11... | collective-permute-start | bytes 98312 | tf_op jit(solution)/shard_map/scores/ppermute | solution.py:403
  41.8 65.1 %copy-start.1 = (f32[2048]{0:T(1024)S(1)}, f32[2048]{0:T(1024)}, u32[]{:S(2)}) copy-start(f32[2048]{0:T(1024)} %param.11) | copy-start | bytes 24580
  41.8 16.4 %collective-permute-start.10 = (bf16[4,8,64,128]{3,2,1,0:T(8,128)(2,1)S(1)}, bf16[4,8,64,128]{3,2,1,0:T(8,128)(2,1)S(1)}, u32[]{:S(2)}, u32[]{:S(2)}) collective-permute-start(bf16[4,8,64,128]{3,2,1,0:T(8,128)(2,1)S(1)} %get-tuple-element.77), channel_id=1, source_target_pairs={{0,2},{2,0},{128,130},{130,128},{1,3},{3,1},{129,131},{131,129},{4... | collective-permute-start | bytes 1572872 | tf_op jit(solution)/shard_map/reduce1/ppermute | solution.py:329
  43.9 16.4 %collective-permute-start.11 = (bf16[4,8,64,128]{3,2,1,0:T(8,128)(2,1)S(1)}, bf16[4,8,64,128]{3,2,1,0:T(8,128)(2,1)S(1)}, u32[]{:S(2)}, u32[]{:S(2)}) collective-permute-start(bf16[4,8,64,128]{3,2,1,0:T(8,128)(2,1)S(1)} %get-tuple-element.78), channel_id=1, source_target_pairs={{64,0},{96,32},{0,64},{32,96},{65,1},{97,33},{1,65},{33,97},{66,2}... | collective-permute-start | bytes 1572872 | tf_op jit(solution)/shard_map/reduce1/ppermute | solution.py:333
  45.1 23.5 %collective-permute-start.12 = (bf16[4,8,64,128]{3,2,1,0:T(8,128)(2,1)S(1)}, bf16[4,8,64,128]{3,2,1,0:T(8,128)(2,1)S(1)}, u32[]{:S(2)}, u32[]{:S(2)}) collective-permute-start(bf16[4,8,64,128]{3,2,1,0:T(8,128)(2,1)S(1)} %get-tuple-element.79), channel_id=1, source_target_pairs={{0,130},{2,128},{128,2},{130,0},{1,131},{3,129},{129,3},{131,1},{4... | collective-permute-start | bytes 1572872 | tf_op jit(solution)/shard_map/reduce1/ppermute | solution.py:329
  46.3 24.1 %collective-permute-start.13 = (bf16[4,8,64,128]{3,2,1,0:T(8,128)(2,1)S(1)}, bf16[4,8,64,128]{3,2,1,0:T(8,128)(2,1)S(1)}, u32[]{:S(2)}, u32[]{:S(2)}) collective-permute-start(bf16[4,8,64,128]{3,2,1,0:T(8,128)(2,1)S(1)} %get-tuple-element.80), channel_id=1, source_target_pairs={{32,0},{64,32},{96,64},{0,96},{33,1},{65,33},{97,65},{1,97},{34,2}... | collective-permute-start | bytes 1572872 | tf_op jit(solution)/shard_map/reduce1/ppermute | solution.py:333
  47.1 23.2 %collective-permute-start.14 = (bf16[4,8,64,128]{3,2,1,0:T(8,128)(2,1)S(1)}, bf16[4,8,64,128]{3,2,1,0:T(8,128)(2,1)S(1)}, u32[]{:S(2)}, u32[]{:S(2)}) collective-permute-start(bf16[4,8,64,128]{3,2,1,0:T(8,128)(2,1)S(1)} %get-tuple-element.81), channel_id=1, source_target_pairs={{0,128},{2,130},{128,0},{130,2},{1,129},{3,131},{129,1},{131,3},{4... | collective-permute-start | bytes 1572872 | tf_op jit(solution)/shard_map/reduce1/ppermute | solution.py:329
  58.2 12.4 %collective-permute-start.15 = (bf16[4,8,64,128]{3,2,1,0:T(8,128)(2,1)S(1)}, bf16[4,8,64,128]{3,2,1,0:T(8,128)(2,1)S(1)}, u32[]{:S(2)}, u32[]{:S(2)}) collective-permute-start(bf16[4,8,64,128]{3,2,1,0:T(8,128)(2,1)S(1)} %get-tuple-element.82), channel_id=1, source_target_pairs={{96,0},{0,32},{32,64},{64,96},{97,1},{1,33},{33,65},{65,97},{98,2}... | collective-permute-start | bytes 1572872 | tf_op jit(solution)/shard_map/reduce1/ppermute | solution.py:333
  71.1 8.0 %collective-permute-start.16 = (bf16[8,64,128]{2,1,0:T(8,128)(2,1)S(1)}, bf16[8,64,128]{2,1,0:T(8,128)(2,1)S(1)}, u32[]{:S(2)}, u32[]{:S(2)}) collective-permute-start(bf16[8,64,128]{2,1,0:T(8,128)(2,1)S(1)} %get-tuple-element.85), channel_id=1, source_target_pairs={{64,0},{96,32},{0,64},{32,96},{65,1},{97,33},{1,65},{33,97},{66,2}... | collective-permute-start | bytes 393224 | tf_op jit(solution)/shard_map/reduce2/ppermute | solution.py:333
  72.4 7.5 %collective-permute-start.17 = (bf16[8,64,128]{2,1,0:T(8,128)(2,1)S(1)}, bf16[8,64,128]{2,1,0:T(8,128)(2,1)S(1)}, u32[]{:S(2)}, u32[]{:S(2)}) collective-permute-start(bf16[8,64,128]{2,1,0:T(8,128)(2,1)S(1)} %get-tuple-element.86), channel_id=1, source_target_pairs={{0,2},{2,0},{128,130},{130,128},{1,3},{3,1},{129,131},{131,129},{4... | collective-permute-start | bytes 393224 | tf_op jit(solution)/shard_map/reduce2/ppermute | solution.py:329
  74.4 6.2 %collective-permute-start.18 = (bf16[8,64,128]{2,1,0:T(8,128)(2,1)S(1)}, bf16[8,64,128]{2,1,0:T(8,128)(2,1)S(1)}, u32[]{:S(2)}, u32[]{:S(2)}) collective-permute-start(bf16[8,64,128]{2,1,0:T(8,128)(2,1)S(1)} %get-tuple-element.87), channel_id=1, source_target_pairs={{32,0},{64,32},{96,64},{0,96},{33,1},{65,33},{97,65},{1,97},{34,2}... | collective-permute-start | bytes 393224 | tf_op jit(solution)/shard_map/reduce2/ppermute | solution.py:333
  75.5 6.2 %collective-permute-start.19 = (bf16[8,64,128]{2,1,0:T(8,128)(2,1)S(1)}, bf16[8,64,128]{2,1,0:T(8,128)(2,1)S(1)}, u32[]{:S(2)}, u32[]{:S(2)}) collective-permute-start(bf16[8,64,128]{2,1,0:T(8,128)(2,1)S(1)} %get-tuple-element.88), channel_id=1, source_target_pairs={{0,130},{2,128},{128,2},{130,0},{1,131},{3,129},{129,3},{131,1},{4... | collective-permute-start | bytes 393224 | tf_op jit(solution)/shard_map/reduce2/ppermute | solution.py:329
  78.1 5.0 %collective-permute-start.20 = (bf16[8,64,128]{2,1,0:T(8,128)(2,1)S(1)}, bf16[8,64,128]{2,1,0:T(8,128)(2,1)S(1)}, u32[]{:S(2)}, u32[]{:S(2)}) collective-permute-start(bf16[8,64,128]{2,1,0:T(8,128)(2,1)S(1)} %get-tuple-element.89), channel_id=1, source_target_pairs={{96,0},{0,32},{32,64},{64,96},{97,1},{1,33},{33,65},{65,97},{98,2}... | collective-permute-start | bytes 393224 | tf_op jit(solution)/shard_map/reduce2/ppermute | solution.py:333
  79.1 5.0 %collective-permute-start.21 = (bf16[8,64,128]{2,1,0:T(8,128)(2,1)S(1)}, bf16[8,64,128]{2,1,0:T(8,128)(2,1)S(1)}, u32[]{:S(2)}, u32[]{:S(2)}) collective-permute-start(bf16[8,64,128]{2,1,0:T(8,128)(2,1)S(1)} %get-tuple-element.90), channel_id=1, source_target_pairs={{0,128},{2,130},{128,0},{130,2},{1,129},{3,131},{129,1},{131,3},{4... | collective-permute-start | bytes 393224 | tf_op jit(solution)/shard_map/reduce2/ppermute | solution.py:329
  84.2 10.1 %collective-permute-start.22 = (f32[128,128]{1,0:T(8,128)S(1)}, f32[128,128]{1,0:T(8,128)S(1)}, u32[]{:S(2)}, u32[]{:S(2)}) collective-permute-start(f32[128,128]{1,0:T(8,128)S(1)} %get-tuple-element.92), channel_id=1, source_target_pairs={{28,0},{0,4},{4,8},{8,12},{12,16},{16,20},{20,24},{24,28},{29,1},{... | collective-permute-start | bytes 196616 | tf_op jit(solution)/shard_map/reduce3/ppermute | solution.py:337
  84.8 13.9 %collective-permute-start.23 = (f32[128,128]{1,0:T(8,128)S(1)}, f32[128,128]{1,0:T(8,128)S(1)}, u32[]{:S(2)}, u32[]{:S(2)}) collective-permute-start(f32[128,128]{1,0:T(8,128)S(1)} %get-tuple-element.93), channel_id=1, source_target_pairs={{4,0},{8,4},{12,8},{16,12},{20,16},{24,20},{28,24},{0,28},{5,1},{9... | collective-permute-start | bytes 196616 | tf_op jit(solution)/shard_map/reduce3/ppermute | solution.py:337
  89.6 13.6 %collective-permute-start.24 = (f32[128,128]{1,0:T(8,128)S(1)}, f32[128,128]{1,0:T(8,128)S(1)}, u32[]{:S(2)}, u32[]{:S(2)}) collective-permute-start(f32[128,128]{1,0:T(8,128)S(1)} %get-tuple-element.94), channel_id=1, source_target_pairs={{24,0},{28,4},{0,8},{4,12},{8,16},{12,20},{16,24},{20,28},{25,1},{... | collective-permute-start | bytes 196616 | tf_op jit(solution)/shard_map/reduce3/ppermute | solution.py:337
  89.8 13.4 %collective-permute-start.25 = (f32[128,128]{1,0:T(8,128)S(1)}, f32[128,128]{1,0:T(8,128)S(1)}, u32[]{:S(2)}, u32[]{:S(2)}) collective-permute-start(f32[128,128]{1,0:T(8,128)S(1)} %get-tuple-element.95), channel_id=1, source_target_pairs={{8,0},{12,4},{16,8},{20,12},{24,16},{28,20},{0,24},{4,28},{9,1},{1... | collective-permute-start | bytes 196616 | tf_op jit(solution)/shard_map/reduce3/ppermute | solution.py:337
  93.7 9.5 %collective-permute-start.26 = (f32[128,128]{1,0:T(8,128)S(1)}, f32[128,128]{1,0:T(8,128)S(1)}, u32[]{:S(2)}, u32[]{:S(2)}) collective-permute-start(f32[128,128]{1,0:T(8,128)S(1)} %get-tuple-element.96), channel_id=1, source_target_pairs={{20,0},{24,4},{28,8},{0,12},{4,16},{8,20},{12,24},{16,28},{21,1},{... | collective-permute-start | bytes 196616 | tf_op jit(solution)/shard_map/reduce3/ppermute | solution.py:337
  94.3 8.9 %collective-permute-start.27 = (f32[128,128]{1,0:T(8,128)S(1)}, f32[128,128]{1,0:T(8,128)S(1)}, u32[]{:S(2)}, u32[]{:S(2)}) collective-permute-start(f32[128,128]{1,0:T(8,128)S(1)} %get-tuple-element.97), channel_id=1, source_target_pairs={{12,0},{16,4},{20,8},{24,12},{28,16},{0,20},{4,24},{8,28},{13,1},{... | collective-permute-start | bytes 196616 | tf_op jit(solution)/shard_map/reduce3/ppermute | solution.py:337
  98.8 8.2 %collective-permute-start.28 = (f32[128,128]{1,0:T(8,128)S(1)}, f32[128,128]{1,0:T(8,128)S(1)}, u32[]{:S(2)}, u32[]{:S(2)}) collective-permute-start(f32[128,128]{1,0:T(8,128)S(1)} %get-tuple-element.98), channel_id=1, source_target_pairs={{16,0},{20,4},{24,8},{28,12},{0,16},{4,20},{8,24},{12,28},{17,1},{... | collective-permute-start | bytes 196616 | tf_op jit(solution)/shard_map/reduce3/ppermute | solution.py:337
